TPU v7x, 256 devices: a whole 4x4x8 slice. The times are simulated.
256 devices in a mesh: row: 8 (over x, z_lo), col: 32 (over z_hi, y, core).
Axes of the slice: x: 4, y: 4, z: 8 (z_hi: 4, z_lo: 2; z = z_hi * 2 + z_lo), core: 2. Of those that a mesh axis runs over, the one named last changes fastest.
Arguments:
- sample_values: float32 [4, 4096], P(None, ('row', 'col')), may hold values from -8 to 8, as said below
- sample_codes: int32 [2, 4096], P(None, ('row', 'col')), may hold values from 0 to 511, as said below
- basis_tables: bfloat16 [2, 512, 12288], P(None, None, 'col'), may hold values from -6 to 6
- model_params: float32 [12288], P('col'), may hold values from -0.0546875 to 0.0546875
- gram_prev: float32 [12288, 12288], P('row', 'col'), may hold values from -6 to 6
- rhs_prev: float32 [12288], P('col'), may hold values from -6 to 6
Outputs:
- gram: float32 [12288, 12288], P('row', 'col')
- rhs: float32 [12288], P('col')
Inputs may be any that keep to these rules, and one draw needn't show every extreme that they name: `sample_values`: row 0 and 1 hold direction cosines within -1 to 1, row 2 a log radius ratio within -0.02 to 0.02, row 3 the observed field. `sample_codes`: row 0 holds grid cell ids, row 1 group indices 0 or 1.
All inputs are finite; a program needn't handle non-finite values.
Results may differ from a plain program's by a relative error of at most 0.0029.
Values may be sent and summed in bfloat16 or wider, within the bound.
A program may use at most 128 MiB of HBM per device.

v0:
```python
import math

import jax
import jax.numpy as jnp
from jax import lax
from jax.sharding import PartitionSpec as P

MAXDEG = 64


def from_root(block, axis, owner):
    block = jnp.where(lax.axis_index(axis) == owner, block, jnp.zeros_like(block))
    return lax.psum(block, axis)


def build_design(tables, cell_ids, geometry, first_col):
    width = tables.shape[2]
    exponent = ((first_col + jnp.arange(width, dtype=jnp.int32)) % MAXDEG + 1).astype(jnp.float32)
    picked = jnp.take(tables, cell_ids, axis=1)
    mixed_part = geometry[0][:, None] * picked[0] + geometry[1][:, None] * picked[1]
    return (mixed_part * jnp.exp(geometry[2][:, None] * exponent[None, :])).astype(jnp.bfloat16)


def local(sample_values, sample_codes, basis_tables, model_params, gram_prev, rhs_prev):
    geometry_all, codes_all = (
        lax.all_gather(sample_values, ("row", "col"), axis=1, tiled=True),
        lax.all_gather(sample_codes, ("row", "col"), axis=1, tiled=True),
    )
    total_rows = geometry_all.shape[1]
    block_rows = min(2048, total_rows)
    blocks = total_rows // block_rows
    col_width = basis_tables.shape[2]
    row_width = gram_prev.shape[0]
    per_row = row_width // col_width
    my_row = lax.axis_index("row")
    my_col = lax.axis_index("col")
    first_col = my_col * col_width
    cell_blocks = codes_all[0].reshape(blocks, block_rows)
    geometry_blocks = jnp.transpose(geometry_all[:3].reshape(3, blocks, block_rows), (1, 0, 2))

    def column_block(packed):
        cell_ids, geometry = packed
        return build_design(basis_tables, cell_ids, geometry, first_col)

    plain_cols = lax.map(column_block, (cell_blocks, geometry_blocks)).reshape(
        total_rows, col_width
    )
    partial_value = jnp.dot(
        plain_cols,
        model_params,
        preferred_element_type=jnp.float32,
        precision=lax.Precision.HIGHEST,
    )
    prediction = lax.psum(partial_value, "col")
    residual = geometry_all[3] - prediction
    group_hot = (codes_all[1][None, :] == jnp.arange(2, dtype=jnp.int32)[:, None]).astype(
        jnp.float32
    )
    counts = jnp.sum(group_hot, axis=1)
    spread = jnp.sum(group_hot * jnp.abs(residual)[None, :], axis=1)
    threshold = 1.345 * spread / jnp.maximum(counts, 1.0)
    limit = jnp.sum(group_hot * threshold[:, None], axis=0)
    weights = limit / jnp.maximum(jnp.abs(residual), limit)
    weighted_cols = (weights[:, None] * plain_cols.astype(jnp.float32)).astype(jnp.bfloat16)
    scale = 1.0 / math.sqrt(total_rows)
    rhs = rhs_prev + scale * jnp.dot(
        residual, weighted_cols, preferred_element_type=jnp.float32, precision=lax.Precision.HIGHEST
    )
    products = []
    for member in range(per_row):
        source_plain = from_root(plain_cols, "col", my_row * per_row + member)
        products.append(
            lax.dot_general(
                source_plain,
                weighted_cols,
                (((0,), (0,)), ((), ())),
                preferred_element_type=jnp.float32,
            )
        )
    gram_new = jnp.concatenate(products, axis=0)
    gram = gram_prev + scale * gram_new
    return (gram, rhs)


def solution(mesh):
    placed = (
        P(None, ("row", "col")),
        P(None, ("row", "col")),
        P(None, None, "col"),
        P("col"),
        P("row", "col"),
        P("col"),
    )
    return jax.shard_map(
        local, mesh=mesh, in_specs=placed, out_specs=(P("row", "col"), P("col")), check_vma=False
    )
```

profile of v0, /device:TPU:17, one launch (start us, length us, event | category | flops | bytes accessed | tf_op | source)
XLA Modules:
  0.0 1112.8 jit_solution(11826525729946261542)
XLA Ops:
  7.2 0.0 copy-start.5
  7.2 0.0 all-reduce.3.cloned.1.call-start
  7.2 343.9 %all-gather.1 = s32[256,16,2]{1,2,0:T(2,128)S(1)} all-gather(s32[1,16,2]{1,2,0:T(2,128)} %bitcast.81), channel_id=1, replica_groups=mesh['row'=8,'col'=32] {'row','col'}, dimensions={0}, use_global_device_ids=true | all-gather | bytes 32896 | tf_op jit(solution)/shard_map/all_gather | solution.py:27
  351.2 0.2 reshape.176
  351.4 0.1 fusion.7
  351.5 340.8 %all-gather = f32[256,16,4]{1,2,0:T(4,128)S(1)} all-gather(f32[1,16,4]{1,2,0:T(4,128)} %bitcast.80), channel_id=1, replica_groups=mesh['row'=8,'col'=32] {'row','col'}, dimensions={0}, use_global_device_ids=true | all-gather | bytes 65792 | tf_op jit(solution)/shard_map/all_gather | solution.py:26
  692.3 0.3 reshape.174
  692.6 0.1 reshape.163
  692.6 0.0 copy-done.5
  692.6 0.8 copy.31
  693.5 51.7 %while.12 = (s32[]{:T(128)}, bf16[2,2048,384]{2,1,0:T(8,128)(2,1)}, f32[2,3,2048]{2,0,1:T(2,128)S(1)}, s32[2,2048]{1,0:T(2,128)S(1)}, bf16[2,512,384]{2,0,1:T(2,...) while((s32[]{:T(128)}, bf16[2,2048,384]{2,1,0:T(8,128)(2,1)}, ...), condition=%wide.region_1.2_spmd, body=%wide.region_0.1_spmd.sunk | while | flops 7890180 | bytes 42606292 | solution.py:45
  693.6 18.8 %gather_fusion = bf16[2048,2,384]{2,1,0:T(2,128)(2,1)} fusion(bf16[2,512,384]{2,0,1:T(2,128)(2,1)S(1)} %get-tuple-element.213, s32[2048]{0:T(1024)S(1)} %broadcast_clamp_fusion.2), kind=kCustom, calls=%fused_computation.clone.1 | custom fusion | bytes 6299648 | tf_op jit(solution)/shard_map/while/body/eval_jaxpr/jit(_take)/gather | solution.py:19
  712.4 2.6 fusion.28
  715.0 0.3 copy-done
  715.2 2.3 fusion.30
  717.6 0.0 copy-start.1
  717.6 1.7 copy-done.1
  719.4 18.8 %gather_fusion = bf16[2048,2,384]{2,1,0:T(2,128)(2,1)} fusion(bf16[2,512,384]{2,0,1:T(2,128)(2,1)S(1)} %get-tuple-element.213, s32[2048]{0:T(1024)S(1)} %broadcast_clamp_fusion.2), kind=kCustom, calls=%fused_computation.clone.1 | custom fusion | bytes 6299648 | tf_op jit(solution)/shard_map/while/body/eval_jaxpr/jit(_take)/gather | solution.py:19
  738.2 2.6 fusion.28
  740.8 0.3 copy-done
  741.1 2.3 fusion.30
  743.4 0.0 copy-start.1
  743.4 1.7 copy-done.1
  745.2 6.1 broadcast_select_fusion.3
  751.2 0.0 all-reduce.3.cloned.1.call-update
  751.3 0.6 copy-done.7
  751.9 4.4 fusion.8
  756.3 134.9 %psum.36 = f32[4096]{0:T(1024)S(1)} all-reduce(f32[4096]{0:T(1024)S(1)} %bitcast.78), channel_id=1, replica_groups=mesh['row'=8,'col'=32] {'col'}, use_global_device_ids=true, to_apply=%region_3.4 | all-reduce | flops 4096 | bytes 32768 | tf_op jit(solution)/shard_map/psum | solution.py:54
  891.2 0.2 select_reduce_fusion.1
  891.4 0.1 select_reduce_fusion
  891.5 2.3 multiply_convert_fusion.1
  893.8 0.0 copy-start.2
  893.8 0.0 copy-start.6
  893.8 1.7 copy-done.2
  895.6 1.3 convolution_reduce_fusion
  896.9 0.0 copy-done.6
  896.9 0.6 multiply_add_fusion
  897.5 196.3 %all-reduce.3.cloned.1.call-done = (bf16[4096,384]{1,0:T(8,128)(2,1)}, bf16[4096,384]{1,0:T(8,128)(2,1)}, bf16[4096,384]{1,0:T(8,128)(2,1)}, bf16[4096,384]{1,0:T(8,128)(2,1)}) async-done(((bf16[4096,384]{1,0:T(8,128)(2,1)}, bf16[4096,384]{1,0:T(8,128)(2,1)}, bf16[4096,384]{1,0:T(8,128)(2,1)}, bf16[4096,384]{1,0:T(8,128)(2,1)}), (bf16[4096,384]{1,0:T(8,128)(2,1)}, bf16[4096,384]{1,0:T(8,128)(2,1)}, ...) | async-done | bytes 12582928 | tf_op jit(solution)/shard_map/psum | solution.py:13
  1093.8 4.8 fusion.12
  1098.6 0.0 copy-done.3
  1098.6 0.0 copy-done.10
  1098.7 0.0 copy-start.9
  1098.7 1.8 fusion.11
  1100.5 0.1 copy-done.9
  1100.5 1.8 fusion.10
  1102.4 0.1 copy-done.8
  1102.4 1.8 fusion.9
  1104.3 1.7 fusion.5
  (27 shorter events, 0.3 us)
Async XLA Ops:
  7.2 685.5 %copy-start.5 = (bf16[2,512,384]{2,1,0:T(8,128)(2,1)S(1)}, bf16[2,512,384]{2,1,0:T(8,128)(2,1)}, u32[]{:S(2)}) copy-start(bf16[2,512,384]{2,1,0:T(8,128)(2,1)} %param.10) | copy-start | bytes 2359300
  7.2 1086.7 %all-reduce.3.cloned.1.call-start = ((), (), s32[]{:S(2)}) async-start(), calls=%async_computation | async-start | bytes 25165824 | tf_op jit(solution)/shard_map/psum | solution.py:13
  712.4 2.8 copy-start
  717.6 1.8 copy-start.1
  738.2 2.8 copy-start
  743.4 1.8 copy-start.1
  751.2 0.7 copy-start.7
  893.8 1.8 copy-start.2
  893.8 3.1 copy-start.6
  1093.8 4.8 copy-start.3
  1093.8 4.8 copy-start.10
  1098.7 1.9 copy-start.9
  1100.5 1.9 copy-start.8
  1102.4 1.8 copy-start.4
Sparse Core Ops, SparseCore 0:
  751.4 342.4 all-reduce.2
where the time goes:
time: 1130 us; the launch traced here: 1110 us
  blocking collectives  820 us (73%)
  waiting for transfers between devices  196 us (17%)
  local copies, waits for them, and re-layouts  45.7 us (4%)
  other arithmetic  20.8 us (2%)
  matrix products  15.9 us (1%)
  between operations  14.2 us (1%)
    all_gather x1, blocking collectives, local(): lax.all_gather(sample_codes, ('row', 'col'), axis=1, tiled=True)  344 us
    all_gather x1, blocking collectives, local(): lax.all_gather(sample_values, ('row', 'col'), axis=1, tiled=True)  341 us
    psum x1, waiting for transfers between devices, from_root(): return lax.psum(block, axis)  196 us
    psum x1, blocking collectives, local(): prediction = lax.psum(partial_value, 'col')  135 us
    gather x2, local copies, waits for them, and re-layouts, build_design(): picked = jnp.take(tables, cell_ids, axis=1)  37.6 us
  transfers between devices with their start and end apart: 1, of which 1 were waited for; matrix products, arithmetic and copies ran while one was open for 1% of the time, Pallas kernels for 0%

commit v1 on v0

v1 whole, which is shorter than its diff:
```python
import functools
import math

import jax
import jax.numpy as jnp
from jax import lax
from jax.experimental import pallas as pl
from jax.experimental.pallas import tpu as pltpu
from jax.sharding import PartitionSpec as P

MAXDEG = 64
MESH = pl.DeviceIdType.MESH
CHUNKS = 4
VMEM_LIMIT = 60 * 1024 * 1024


def exchange_kernel(
    nrow, ncol, width,
    basis_ref, params_ref, samp_ref,
    rows_ref, own_ref, sums_ref, samples_ref,
    part, land1, slot1, tot1, land2, slot2,
    send1, recv1, send2, recv2, send3, recv3,
    sends, recvs, local_sem, stage_recv, fwd_recv, mate_recv, core_recv, fwd_send, stage_send,
):
    nz = ncol // 8
    row, col = lax.axis_index("row"), lax.axis_index("col")
    x, zlo = row // 2, row % 2
    zhi, yk = col // 8, col % 8
    y, core = yk // 2, yk % 2
    ncell = basis_ref.shape[1]
    lanes = sums_ref.shape[2]
    rows_chunk = width // CHUNKS

    def col_of(zh, yy, kk):
        return zh * 8 + yy * 2 + kk

    owner = (y // 2) == zlo
    mate_y = y + 1 - 2 * (y % 2)
    outer_y = (y + 3 + 2 * (y % 2)) % 4
    mate = (row, col_of(zhi, mate_y, core))
    outer = (row, col_of(zhi, outer_y, core))
    sibling = (row, col_of(zhi, y, 1 - core))
    target = (2 * zhi + y // 2, col_of(x, y, core))
    to_self = (zhi == x) & owner
    parity = y % 2
    mine = jnp.where(owner, parity, 1 - parity)
    slot_mine = 2 * mine + core
    slot_mate = 2 * (1 - mine) + core

    barrier = pltpu.get_barrier_semaphore()

    def greet(device):
        pl.semaphore_signal(barrier, inc=1, device_id=device, device_id_type=MESH)

    for d in range(1, 8):
        greet((row, zhi * 8 + (yk + d) % 8))
    for d in range(1, nz):
        greet((row, ((zhi + d) % nz) * 8 + yk))
    for d in range(1, nrow):
        greet(((row + d) % nrow, col))
    for half in range(2):
        @pl.when(owner & ((zhi != x) | (zlo != half)))
        def _():
            greet((2 * zhi + half, col_of(x, y, core)))

    for a in range(2):
        total = None
        for j in range(width // 128):
            block = basis_ref[a, :, 128 * j : 128 * (j + 1)].astype(jnp.float32)
            turned = block.T
            own_ref[128 * j : 128 * (j + 1), a * ncell : (a + 1) * ncell] = turned.astype(jnp.bfloat16)
            term = block * params_ref[:, 128 * j : 128 * (j + 1)]
            total = term if total is None else total + term
        turned = total.T
        both = turned[:MAXDEG] + turned[MAXDEG:]
        per = ncell // lanes
        for i in range(per):
            part[a * per + i] = both[:, i * lanes : (i + 1) * lanes]

    count = 7 + (nz - 1) + (nrow - 1)
    pl.semaphore_wait(barrier, count + 1 - to_self.astype(jnp.int32))

    def remote(src, dst, ssem, rsem, device):
        return pltpu.make_async_remote_copy(
            src_ref=src, dst_ref=dst, send_sem=ssem, recv_sem=rsem, device_id=device, device_id_type=MESH
        )

    first = []
    for d in range(1, 8):
        peer = (row, zhi * 8 + (yk + d) % 8)
        first.append(remote(part.at[row], land1.at[d], send1.at[d], recv1.at[d], peer))
        first.append(remote(samp_ref, slot1.at[yk], sends.at[d], recvs.at[d], peer))
    for copy in first:
        copy.start()

    def table(slot, j):
        return rows_ref.at[slot, pl.ds(rows_chunk * j, rows_chunk)]

    per_half = CHUNKS // 2
    for j in range(CHUNKS):
        half = j // per_half
        source = own_ref.at[pl.ds(rows_chunk * j, rows_chunk)]

        @pl.when((zlo == half) & jnp.logical_not(to_self))
        def _():
            remote(source, table(2 * parity + core, j), stage_send.at[j], stage_recv.at[j], target).start()

        @pl.when((zlo == half) & to_self)
        def _():
            pltpu.make_async_copy(source, table(2 * parity + core, j), stage_recv.at[j]).start()

    slot1[yk] = samp_ref[...]
    for copy in first:
        copy.wait_recv()
    total = part[row]
    for d in range(1, 8):
        total = total + land1[d]
    tot1[...] = total
    for i in range(8):
        slot2[zhi, pl.ds(i, 1)] = slot1[i]

    second = []
    for d in range(1, nz):
        peer = (row, ((zhi + d) % nz) * 8 + yk)
        second.append(remote(tot1, land2.at[d], send2.at[d], recv2.at[d], peer))
        second.append(remote(slot2.at[zhi], slot2.at[zhi], sends.at[7 + d], recvs.at[7 + d], peer))
    for copy in second:
        copy.start()

    def got(j):
        return remote(table(slot_mine, j), table(slot_mine, j), fwd_send.at[0, j], fwd_recv.at[j], mate)

    def pass_mine(j):
        @pl.when(owner)
        def _():
            pltpu.make_async_copy(
                own_ref.at[pl.ds(rows_chunk * j, rows_chunk)], table(slot_mine, j), stage_recv.at[j]
            ).wait()

        @pl.when(jnp.logical_not(owner))
        def _():
            got(j).wait_recv()

        remote(table(slot_mine, j), table(slot_mine, j), fwd_send.at[0, j], mate_recv.at[j], mate).start()

        @pl.when(owner)
        def _():
            remote(table(slot_mine, j), table(slot_mine, j), fwd_send.at[1, j], fwd_recv.at[j], outer).start()

        remote(table(slot_mine, j), table(slot_mine, j), fwd_send.at[2, j], core_recv.at[0, j], sibling).start()

    def pass_mate(j):
        remote(table(slot_mate, j), table(slot_mate, j), fwd_send.at[0, j], mate_recv.at[j], mate).wait_recv()
        remote(table(slot_mate, j), table(slot_mate, j), fwd_send.at[3, j], core_recv.at[1, j], sibling).start()

    pass_mine(0)

    for copy in second:
        copy.wait_recv()
    total = tot1[...]
    for d in range(1, nz):
        total = total + land2[d]
    sums_ref[row] = total
    for i in range(nz):
        samples_ref[row, pl.ds(8 * i, 8)] = slot2[i]

    third = []
    for d in range(1, nrow):
        peer = ((row + d) % nrow, col)
        third.append(remote(sums_ref.at[row], sums_ref.at[row], send3.at[d], recv3.at[d], peer))
        third.append(remote(samples_ref.at[row], samples_ref.at[row], sends.at[10 + d], recvs.at[10 + d], peer))
    for copy in third:
        copy.start()

    for j in range(1, CHUNKS):
        pass_mine(j)
        pass_mate(j - 1)
    pass_mate(CHUNKS - 1)

    for copy in third:
        copy.wait_recv()
    for j in range(CHUNKS):
        remote(table(0, j), table(0, j), fwd_send.at[2, j], core_recv.at[0, j], sibling).wait_recv()
        remote(table(0, j), table(0, j), fwd_send.at[3, j], core_recv.at[1, j], sibling).wait_recv()

    for copy in first + second + third:
        copy.wait_send()
    for j in range(CHUNKS):
        @pl.when((zlo == j // per_half) & jnp.logical_not(to_self))
        def _():
            remote(table(0, j), table(0, j), stage_send.at[j], stage_recv.at[j], target).wait_send()

        for kind in (0, 2, 3):
            remote(table(0, j), table(0, j), fwd_send.at[kind, j], fwd_recv.at[j], mate).wait_send()

        @pl.when(owner)
        def _():
            remote(table(0, j), table(0, j), fwd_send.at[1, j], fwd_recv.at[j], outer).wait_send()


def exchange(nrow, ncol, tables, params, packed):
    ncell, width = tables.shape[1:]
    lanes = 2 * ncell // nrow
    nz = ncol // 8
    dma = pltpu.SemaphoreType.DMA
    vmem = pl.BlockSpec(memory_space=pltpu.VMEM)
    f32, bf16 = jnp.float32, jnp.bfloat16
    return pl.pallas_call(
        functools.partial(exchange_kernel, nrow, ncol, width),
        out_shape=(
            jax.ShapeDtypeStruct((4, width, 2 * ncell), bf16),
            jax.ShapeDtypeStruct((width, 2 * ncell), bf16),
            jax.ShapeDtypeStruct((nrow, MAXDEG, lanes), f32),
            jax.ShapeDtypeStruct((nrow, ncol, 128), f32),
        ),
        in_specs=[vmem] * 3,
        out_specs=(vmem,) * 4,
        scratch_shapes=[
            pltpu.VMEM((nrow, MAXDEG, lanes), f32),
            pltpu.VMEM((8, MAXDEG, lanes), f32),
            pltpu.VMEM((8, 1, 128), f32),
            pltpu.VMEM((MAXDEG, lanes), f32),
            pltpu.VMEM((nz, MAXDEG, lanes), f32),
            pltpu.VMEM((nz, 8, 128), f32),
            dma((8,)), dma((8,)),
            dma((nz,)), dma((nz,)),
            dma((nrow,)), dma((nrow,)),
            dma((20,)), dma((20,)),
            dma, dma((CHUNKS,)), dma((CHUNKS,)), dma((CHUNKS,)), dma((2, CHUNKS)), dma((4, CHUNKS)), dma((CHUNKS,)),
        ],
        compiler_params=pltpu.CompilerParams(
            collective_id=0, has_side_effects=True, vmem_limit_bytes=VMEM_LIMIT
        ),
    )(tables, params, packed)


TILE = 256


def normal_kernel(
    scale,
    rows_ref, own_ref, sums_ref, samples_ref, gram_prev_ref, rhs_prev_ref,
    gram_ref, rhs_ref,
    turned, pieces, grown, hots, pred, design, weighted, plain, extra,
):
    f32, bf16 = jnp.float32, jnp.bfloat16
    ncell = rows_ref.shape[2] // 2
    width = own_ref.shape[0]
    ndev = samples_ref.shape[0]
    nrow, _, lanes = sums_ref.shape
    tiles = pred.shape[0]
    per = nrow // 2
    turned[...] = samples_ref[...].T
    for a in range(2):
        for i in range(per):
            value = sums_ref[a * per + i]
            for n in range(3):
                piece = value.astype(bf16)
                pieces[a, n * MAXDEG : (n + 1) * MAXDEG, i * lanes : (i + 1) * lanes] = piece
                value = value - piece.astype(f32)

    exponent = (lax.broadcasted_iota(jnp.int32, (MAXDEG, TILE), 0) + 1).astype(f32)
    cells = lax.broadcasted_iota(jnp.int32, (ncell, TILE), 0)

    def field(number, k):
        return turned[pl.ds(number * tiles + k, 1), :]

    def prepare(k, carry):
        grow = jnp.exp(field(2, k) * exponent)
        grown[0, k] = grow * field(0, k)
        grown[1, k] = grow * field(1, k)
        hot = (cells == field(4, k).astype(jnp.int32)).astype(f32).astype(bf16)
        hots[k] = hot
        value = None
        for a in range(2):
            picked = jnp.dot(pieces[a], hot, preferred_element_type=f32)
            term = grown[a, k] * (
                picked[:MAXDEG] + picked[MAXDEG : 2 * MAXDEG] + picked[2 * MAXDEG :]
            )
            value = term if value is None else value + term
        pred[pl.ds(k, 1), :] = jnp.sum(value, axis=0, keepdims=True)
        return carry

    lax.fori_loop(0, tiles, prepare, 0)

    residual = turned[3 * tiles : 4 * tiles, :] - pred[...]
    group = turned[5 * tiles : 6 * tiles, :]
    size = jnp.abs(residual)
    limit = jnp.zeros_like(size)
    for number in range(2):
        hot = (group == float(number)).astype(f32)
        count = jnp.sum(jnp.sum(hot, axis=0, keepdims=True), axis=1, keepdims=True)
        spread = jnp.sum(jnp.sum(hot * size, axis=0, keepdims=True), axis=1, keepdims=True)
        limit = limit + hot * (1.345 * spread / jnp.maximum(count, 1.0))
    weights = limit / jnp.maximum(size, limit)
    turned[3 * tiles : 4 * tiles, :] = residual
    turned[5 * tiles : 6 * tiles, :] = weights

    def build(k, carry):
        hot = hots[k]
        first, second = grown[0, k], grown[1, k]
        at = pl.ds(pl.multiple_of(k * TILE, TILE), TILE)

        def designed(table):
            east = jnp.dot(table[:, :ncell], hot, preferred_element_type=f32)
            north = jnp.dot(table[:, ncell:], hot, preferred_element_type=f32)
            return [
                (
                    east[MAXDEG * i : MAXDEG * (i + 1)] * first
                    + north[MAXDEG * i : MAXDEG * (i + 1)] * second
                ).astype(bf16)
                for i in range(table.shape[0] // MAXDEG)
            ]

        weight = field(5, k)
        for i, block in enumerate(designed(own_ref[...])):
            weighted[MAXDEG * i : MAXDEG * (i + 1), at] = (block.astype(f32) * weight).astype(bf16)
        for t in range(4):
            for i, block in enumerate(designed(rows_ref[t])):
                design[pl.ds(t * width + MAXDEG * i, MAXDEG), at] = block
        value = field(3, k)
        for n in range(3):
            piece = value.astype(bf16).astype(f32)
            extra[pl.ds(n, 1), at] = piece
            value = value - piece
        return carry

    extra[...] = jnp.zeros_like(extra)
    lax.fori_loop(0, tiles, build, 0)

    nt = (((1,), (1,)), ((), ()))

    def gram_step(i, carry):
        at = pl.ds(pl.multiple_of(i * width, width), width)
        product = lax.dot_general(design[at, :], weighted[...], nt, preferred_element_type=f32)
        gram_ref[at, :] = gram_prev_ref[at, :] + scale * product
        return carry

    lax.fori_loop(0, 4, gram_step, 0)
    side = lax.dot_general(extra[...].astype(bf16), weighted[...], nt, preferred_element_type=f32)
    rhs_ref[...] = rhs_prev_ref[...] + scale * jnp.sum(side[:8], axis=0, keepdims=True)


def normal(tables_rows, table_own, sums, samples, gram_prev, rhs_prev):
    f32, bf16 = jnp.float32, jnp.bfloat16
    ndev = samples.shape[0]
    tiles = samples.shape[0] * 16 // TILE
    total = tiles * TILE
    ncell = table_own.shape[1] // 2
    width = table_own.shape[0]
    vmem = pl.BlockSpec(memory_space=pltpu.VMEM)
    return pl.pallas_call(
        functools.partial(normal_kernel, 1.0 / math.sqrt(total)),
        out_shape=(
            jax.ShapeDtypeStruct(gram_prev.shape, f32),
            jax.ShapeDtypeStruct(rhs_prev.shape, f32),
        ),
        in_specs=[vmem] * 6,
        out_specs=(vmem, vmem),
        scratch_shapes=[
            pltpu.VMEM((128, ndev), f32),
            pltpu.VMEM((2, 3 * MAXDEG, ncell), bf16),
            pltpu.VMEM((2, tiles, MAXDEG, TILE), f32),
            pltpu.VMEM((tiles, ncell, TILE), bf16),
            pltpu.VMEM((tiles, TILE), f32),
            pltpu.VMEM((4 * width, total), bf16),
            pltpu.VMEM((width, total), bf16),
            pltpu.VMEM((8, 128), f32),
            pltpu.VMEM((16, total), f32),
        ],
        compiler_params=pltpu.CompilerParams(vmem_limit_bytes=VMEM_LIMIT),
    )(tables_rows, table_own, sums, samples, gram_prev, rhs_prev)


def local(nrow, ncol, sample_values, sample_codes, basis_tables, model_params, gram_prev, rhs_prev):
    width = basis_tables.shape[2]
    packed = jnp.concatenate(
        [
            sample_values.reshape(1, -1),
            sample_codes.astype(jnp.float32).reshape(1, -1),
            jnp.zeros((1, 32), jnp.float32),
        ],
        axis=1,
    )
    rows, own, sums, samples = exchange(nrow, ncol, basis_tables, model_params.reshape(1, width), packed)
    gram, rhs = normal(rows, own, sums, samples.reshape(nrow * ncol, 128), gram_prev, rhs_prev.reshape(1, width))
    return (gram, rhs.reshape(width))


def solution(mesh):
    placed = (
        P(None, ("row", "col")),
        P(None, ("row", "col")),
        P(None, None, "col"),
        P("col"),
        P("row", "col"),
        P("col"),
    )
    return jax.shard_map(
        functools.partial(local, mesh.shape["row"], mesh.shape["col"]),
        mesh=mesh,
        in_specs=placed,
        out_specs=(P("row", "col"), P("col")),
        check_vma=False,
    )
```

time: 1130 us -> 116 us (0.10); the launches traced: 1110 us -> 116 us
  blocking collectives: 820 us -> 0 us
  waiting for transfers between devices: 196 us -> 0 us
  Pallas kernels: 0 us -> 109 us
  local copies, waits for them, and re-layouts: 45.7 us -> 3.32 us
  other arithmetic: 20.8 us -> 2.52 us
  matrix products: 15.9 us -> 0 us
  between operations: 14.2 us -> 0.64 us
    all_gather x2 -> x0, blocking collectives: 685 us -> none  [the longest x1 344 us: local(): lax.all_gather(sample_codes, ('row', 'col'), axis=1, tiled=True)]
    psum x1 -> x0, waiting for transfers between devices: 196 us -> none  [from_root(): return lax.psum(block, axis)]
    psum x1 -> x0, blocking collectives: 135 us -> none  [local(): prediction = lax.psum(partial_value, 'col')]
    pallas_call x0 -> x2, Pallas kernels: none -> 109 us  [the longest x1 73.2 us: exchange(): pl.pallas_call(functools.partial(exchange_kernel, nrow, ncol, width), out...]
    gather x2 -> x0, local copies, waits for them, and re-layouts: 37.6 us -> none  [build_design(): picked = jnp.take(tables, cell_ids, axis=1)]
    dot_general x6 -> x0, matrix products: 15.9 us -> none  [the longest x4 10.2 us: local(): lax.dot_general(source_plain, weighted_cols, (((0,), (0,)), ((), ())), pr...]
  transfers between devices with their start and end apart: 1 -> 0, of which waited for: 1 -> 0; matrix products, arithmetic and copies ran while one was open for 1% -> 0% of each run, Pallas kernels for 0% -> 0%
where the time goes in v1:
time: 116 us
  Pallas kernels  109 us (94%)
  local copies, waits for them, and re-layouts  3.32 us (3%)
  other arithmetic  2.52 us (2%)
    pallas_call x1, Pallas kernels, exchange(): pl.pallas_call(functools.partial(exchange_kernel, nrow, ncol, width), out...  73.2 us
    pallas_call x1, Pallas kernels, normal(): pl.pallas_call(functools.partial(normal_kernel, 1.0 / math.sqrt(total)),...  36 us

profile of v1, /device:TPU:17, one launch (start us, length us, event | category | flops | bytes accessed | tf_op | source)
XLA Modules:
  0.0 115.7 jit_solution(5988076400592749260)
XLA Ops:
  0.6 0.8 reshape.23
  1.4 0.7 convert_element_type.3
  2.1 0.1 reshape.24
  2.2 0.6 bitcast_maximum_fusion.samp_ref
  2.8 1.2 %reshape.22.params_ref = f32[1,384]{1,0:T(1,128)} reshape(f32[384]{0:T(512)} %param.9) | data formatting | bytes 3072 | tf_op jit(solution)/shard_map/reshape | solution.py:385
  4.0 1.2 %reshape.26.rhs_prev_ref = f32[1,384]{1,0:T(1,128)} reshape(f32[384]{0:T(512)} %param.11) | data formatting | bytes 3072 | tf_op jit(solution)/shard_map/reshape | solution.py:386
  5.2 73.2 %shard_map.77 = (bf16[4,384,1024]{2,1,0:T(8,128)(2,1)}, bf16[384,1024]{1,0:T(8,128)(2,1)}, f32[8,64,128]{2,1,0:T(8,128)}, f32[8,32,128]{2,1,0:T(8,128)}) custom-call(bf16[2,512,384]{2,1,0:T(8,128)(2,1)} %basis_ref.1, f32[1,384]{1,0:T(1,128)} %reshape.22.params_ref, f32[1,128]{1,0:T(1,128)} %bitcast_maximum_fusion.samp_ref), custom_call_target="tpu_custom_call" | custom-call | tf_op jit(solution)/shard_map/pallas_call | solution.py:208
  78.4 36.0 %shard_map.78 = (f32[1536,384]{1,0:T(8,128)}, f32[1,384]{1,0:T(1,128)}) custom-call(bf16[4,384,1024]{2,1,0:T(8,128)(2,1)} %get-tuple-element.8.rows_ref, bf16[384,1024]{1,0:T(8,128)(2,1)} %get-tuple-element.9.own_ref, f32[8,64,128]{2,1,0:T(8,128)} %get-tuple-element.10.sums_ref, f32[256,128]{1,0:T(8,128)} %bitcast.3, f32[1536,384]{1,0:T(8,128)} %gram_prev_ref.1, ...), custom_call_target="tpu_custom_call" | custom-call | tf_op jit(solution)/shard_map/pallas_call | solution.py:352
  114.4 1.2 %reduce = f32[384]{0:T(512)} reduce(f32[1,384]{1,0:T(1,128)} %get-tuple-element.13, f32[]{:T(128)} %constant.4), dimensions={0}, to_apply=%get-tuple-element.13.reduce_sub_computation | reduce | bytes 3076 | tf_op jit(solution)/shard_map/pallas_call | solution.py:352
  (1 shorter events, 0.0 us)

commit v2 on v0

v2 whole, which is shorter than its diff:
```python
import functools
import math

import jax
import jax.numpy as jnp
from jax import lax
from jax.experimental import pallas as pl
from jax.experimental.pallas import tpu as pltpu
from jax.sharding import PartitionSpec as P

MAXDEG = 64
MESH = pl.DeviceIdType.MESH
VMEM_LIMIT = 60 * 1024 * 1024
NT = (((1,), (1,)), ((), ()))
SIDE = 16


def kernel(
    nrow, ncol,
    basis_ref, params_ref, values_ref, codes_ref, prev_ref, rhs_prev_ref,
    gram_ref, rhs_ref,
    own, tab, zbuf, part, land1, tot1, land2, sums, slots, samples,
    turned, pieces, grown, hots, pred, design, weighted, gram, away, back,
    s1_send, s1_recv, s2_send, s2_recv,
    g1_send, g1_recv, g2_send, g2_recv, g3_send, g3_recv,
    z_send, z_recv, x_send, x_recv, y_send, outer_recv, mate_recv,
    w_send, w_recv, p_send, p_recv, prev_sem, out_sem,
):
    f32, bf16 = jnp.float32, jnp.bfloat16
    nz = ncol // 8
    row, col = lax.axis_index("row"), lax.axis_index("col")
    x, zlo = row // 2, row % 2
    zhi, yk = col // 8, col % 8
    y, core = yk // 2, yk % 2
    ncell, width = basis_ref.shape[1:]
    lanes = sums.shape[2]
    piece = width // nrow
    tiles = values_ref.shape[1]
    tile = nrow * ncol
    total = tiles * tile
    scale = 1.0 / math.sqrt(total)

    def remote(src, dst, ssem, rsem, device):
        return pltpu.make_async_remote_copy(
            src_ref=src, dst_ref=dst, send_sem=ssem, recv_sem=rsem, device_id=device, device_id_type=MESH
        )

    owner = (y // 2) == zlo
    mate = (row, zhi * 8 + 2 * (y + 1 - 2 * (y % 2)) + core)
    outer = (row, zhi * 8 + 2 * ((y + 3 + 2 * (y % 2)) % 4) + core)
    sibling = (row, zhi * 8 + 2 * y + 1 - core)
    col_peers = [(row, (col + d) % ncol) for d in range(ncol)]
    row_peers = [((row + d) % nrow, col) for d in range(nrow)]
    near = [(row, zhi * 8 + (yk + d) % 8) for d in range(8)]
    far = [(row, ((zhi + d) % nz) * 8 + yk) for d in range(nz)]
    other = row + 1 - 2 * zlo
    hand = [(other, far[d][1]) if 2 * d == nz else far[d] for d in range(nz)]
    handed = [other if 2 * d == nz else row for d in range(nz)]
    parity = y % 2
    mine = jnp.where(owner, parity, 1 - parity)

    barrier = pltpu.get_barrier_semaphore()
    greeted = col_peers[1:] + row_peers[1:] + [hand[d] for d in range(1, nz) if 2 * d == nz]
    for peer in greeted:
        pl.semaphore_signal(barrier, inc=1, device_id=peer, device_id_type=MESH)

    prev_copy = pltpu.make_async_copy(prev_ref, gram, prev_sem)
    prev_copy.start()

    slots[row] = jnp.concatenate(
        [values_ref[i : i + 1, :] for i in range(4)]
        + [codes_ref[i : i + 1, :].astype(f32) for i in range(2)]
        + [jnp.zeros((1, 128 - 6 * tiles), f32)],
        axis=1,
    )
    params = params_ref[...].reshape(1, width)
    for a in range(2):
        turns = []
        amount = None
        for j in range(width // 128):
            block = basis_ref[a, :, 128 * j : 128 * (j + 1)].astype(f32)
            turns.append(block.T)
            term = block * params[:, 128 * j : 128 * (j + 1)]
            amount = term if amount is None else amount + term
        whole = jnp.concatenate(turns, axis=0).astype(bf16)
        for p in range(nrow):
            own[p, a * piece : (a + 1) * piece, :] = whole[piece * p : piece * (p + 1)]
        amount = amount.T
        amount = amount[:MAXDEG] + amount[MAXDEG:]
        per = ncell // lanes
        for i in range(per):
            part[a * per + i] = amount[:, i * lanes : (i + 1) * lanes]

    pl.semaphore_wait(barrier, len(greeted))

    s1 = [remote(slots.at[row], slots.at[row], s1_send.at[d], s1_recv.at[d], row_peers[d]) for d in range(1, nrow)]
    for copy in s1:
        copy.start()

    zs = [remote(own.at[row], zbuf.at[nz - d], z_send.at[d], z_recv.at[nz - d], hand[d]) for d in range(1, nz)]
    for copy in zs:
        copy.start()

    def pass_x(d):
        to = 2 * ((zhi + d) % nz) + y // 2
        source = own.at[row] if d == 0 else zbuf.at[d]
        i = (handed[d] - to + nrow) % nrow
        place = tab.at[i, parity]

        @pl.when(to != row)
        def _():
            remote(source, place, x_send.at[d], x_recv.at[i], (to, col)).start()

        @pl.when(to == row)
        def _():
            pltpu.make_async_copy(source, place, x_recv.at[i]).start()

    pass_x(0)
    g1 = [remote(part.at[row], land1.at[d], g1_send.at[d], g1_recv.at[d], near[d]) for d in range(1, 8)]
    for copy in g1:
        copy.start()

    for copy in s1:
        copy.wait_recv()
    for i in range(nrow):
        samples[col, pl.ds(i, 1)] = slots[i]
    s2 = [
        remote(samples.at[col], samples.at[col], s2_send.at[d], s2_recv.at[d], col_peers[d]) for d in range(1, ncol)
    ]
    for copy in s2:
        copy.start()

    for d in range(1, nz):
        remote(zbuf.at[d], zbuf.at[d], z_send.at[d], z_recv.at[d], hand[d]).wait_recv()
        pass_x(d)

    def pass_y(i):
        here = tab.at[i, mine]

        @pl.when(owner)
        def _():
            pltpu.make_async_copy(here, here, x_recv.at[i]).wait()
            remote(here, here, y_send.at[1, i], outer_recv.at[i], outer).start()

        @pl.when(jnp.logical_not(owner))
        def _():
            remote(here, here, y_send.at[1, i], outer_recv.at[i], outer).wait_recv()

        remote(here, here, y_send.at[0, i], mate_recv.at[i], mate).start()

    def wait_mate(i):
        here = tab.at[i, 1 - mine]
        remote(here, here, y_send.at[0, i], mate_recv.at[i], mate).wait_recv()

    def field(number, k):
        return turned[pl.ds(number * tiles + k, 1), :]

    def span(k):
        return pl.ds(pl.multiple_of(k * tile, tile), tile)

    exponent = (lax.broadcasted_iota(jnp.int32, (MAXDEG, tile), 0) + 1).astype(f32)
    cells = lax.broadcasted_iota(jnp.int32, (ncell, tile), 0)
    reach = grown.shape[2]

    def prepare(k, carry):
        grow = jnp.exp(field(2, k) * exponent)
        for a in range(2):
            value = grow * field(a, k)
            for first in range(0, reach, MAXDEG):
                size = min(MAXDEG, reach - first)
                grown[a, k, first : first + size] = value[:size]
        hots[k] = (cells == field(4, k).astype(jnp.int32)).astype(f32).astype(bf16)
        return carry

    def mixed(picked, k, p):
        at = pl.ds(pl.multiple_of((p * piece) % MAXDEG, 16), piece)
        return (picked[:piece] * grown[0, k, at] + picked[piece:] * grown[1, k, at]).astype(bf16)

    def build_own(k, carry):
        picked = jnp.dot(own[...].reshape(2 * width, ncell), hots[k], preferred_element_type=f32)
        for p in range(nrow):
            weighted[0, p * piece : (p + 1) * piece, span(k)] = mixed(
                picked[2 * piece * p : 2 * piece * (p + 1)], k, p
            )
        return carry

    def predict(k, carry):
        value = None
        for a in range(2):
            picked = jnp.dot(pieces[a], hots[k], preferred_element_type=f32)
            term = grown[a, k, :MAXDEG] * (
                picked[:MAXDEG] + picked[MAXDEG : 2 * MAXDEG] + picked[2 * MAXDEG :]
            )
            value = term if value is None else value + term
        pred[pl.ds(k, 1), :] = jnp.sum(value, axis=0, keepdims=True)
        return carry

    def weigh(k, carry):
        weighted[0, :, span(k)] = (weighted[0, :, span(k)].astype(f32) * field(5, k)).astype(bf16)
        rest = field(3, k)
        split = []
        for n in range(3):
            split.append(rest.astype(bf16).astype(f32))
            rest = rest - split[-1]
        split.append(jnp.zeros((SIDE - 3, tile), f32))
        design[width : width + SIDE, span(k)] = jnp.concatenate(split, axis=0).astype(bf16)
        return carry

    step = max(1, nrow // 4)

    def build_rows(unit):
        def body(k, carry):
            lhs = tab[step * unit : step * (unit + 1)].reshape(step * 4 * piece, ncell)
            picked = jnp.dot(lhs, hots[k], preferred_element_type=f32)
            for n in range(step):
                i = step * unit + n
                for par in range(2):
                    first = (2 * n + par) * 2 * piece
                    at = (2 * i + par) * piece + (SIDE if 2 * i >= nrow else 0)
                    design[at : at + piece, span(k)] = mixed(
                        picked[first : first + 2 * piece], k, (row + i) % nrow
                    )
            return carry

        lax.fori_loop(0, tiles, body, 0, unroll=2)

    def place(i, par, which):
        return pl.ds(pl.multiple_of((2 * par + which) * width + ((row + i) % nrow) * piece, 16), piece)

    def out_copy(i, par, which):
        at = place(i, par, which)
        return pltpu.make_async_copy(gram.at[at], gram_ref.at[at], out_sem.at[i, par, which])

    half = nrow // 2

    def form(h):
        rows = width + (SIDE if h == 0 else 0)
        first = 0 if h == 0 else width + SIDE
        both = weighted[...].reshape(2 * width, total)
        product = lax.dot_general(design[first : first + rows], both, NT, preferred_element_type=f32)
        away[h] = product[:width, width:]
        remote(away.at[h], back.at[h], p_send.at[h], p_recv.at[h], sibling).start()
        for n in range(half):
            for par in range(2):
                at = place(half * h + n, par, core)
                begin = (2 * n + par) * piece
                gram[at, :] = gram[at, :] + scale * product[begin : begin + piece, :width]
                out_copy(half * h + n, par, core).start()
        if h == 0:
            rhs_ref[...] = rhs_prev_ref[...] + scale * jnp.sum(product[width : width + 8, :width], axis=0)

    def finish(h):
        remote(away.at[h], back.at[h], p_send.at[h], p_recv.at[h], sibling).wait_recv()
        for n in range(half):
            for par in range(2):
                at = place(half * h + n, par, 1 - core)
                begin = (2 * n + par) * piece
                gram[at, :] = gram[at, :] + scale * back[h, begin : begin + piece, :]
                out_copy(half * h + n, par, 1 - core).start()

    def some(body, number, parts):
        lax.fori_loop(number * tiles // parts, (number + 1) * tiles // parts, body, 0, unroll=2)

    pass_y(0)
    for copy in g1:
        copy.wait_recv()
    amount = part[row]
    for d in range(1, 8):
        amount = amount + land1[d]
    tot1[...] = amount
    g2 = [remote(tot1, land2.at[d], g2_send.at[d], g2_recv.at[d], far[d]) for d in range(1, nz)]
    for copy in g2:
        copy.start()

    for copy in s2:
        copy.wait_recv()
    turned[...] = samples[...].reshape(tile, 128).T
    for n in range(4):
        some(prepare, n, 4)
        if n + 1 < nrow:
            pass_y(n + 1)
        if n == 1:
            for copy in g2:
                copy.wait_recv()
            amount = tot1[...]
            for d in range(1, nz):
                amount = amount + land2[d]
            sums[row] = amount
            g3 = [
                remote(sums.at[row], sums.at[row], g3_send.at[d], g3_recv.at[d], row_peers[d])
                for d in range(1, nrow)
            ]
            for copy in g3:
                copy.start()
    for n in range(4):
        some(build_own, n, 4)
        if n + 5 < nrow:
            pass_y(n + 5)

    for copy in g3:
        copy.wait_recv()
    per = nrow // 2
    for a in range(2):
        for i in range(per):
            value = sums[a * per + i]
            for n in range(3):
                part_value = value.astype(bf16)
                pieces[a, n * MAXDEG : (n + 1) * MAXDEG, i * lanes : (i + 1) * lanes] = part_value
                value = value - part_value.astype(f32)
    some(predict, 0, 1)

    residual = turned[3 * tiles : 4 * tiles, :] - pred[...]
    group = turned[5 * tiles : 6 * tiles, :]
    size = jnp.abs(residual)
    limit = jnp.zeros_like(size)
    for number in range(2):
        hot = (group == float(number)).astype(f32)
        count = jnp.sum(jnp.sum(hot, axis=0, keepdims=True), axis=1, keepdims=True)
        spread = jnp.sum(jnp.sum(hot * size, axis=0, keepdims=True), axis=1, keepdims=True)
        limit = limit + hot * (1.345 * spread / jnp.maximum(count, 1.0))
    turned[3 * tiles : 4 * tiles, :] = residual
    turned[5 * tiles : 6 * tiles, :] = limit / jnp.maximum(size, limit)
    some(weigh, 0, 1)
    w_copy = remote(weighted.at[0], weighted.at[1], w_send, w_recv, sibling)
    w_copy.start()

    units = nrow // step
    for unit in range(units):
        for i in range(step * unit, step * (unit + 1)):
            wait_mate(i)
        build_rows(unit)
        if unit + 1 == units // 2:
            w_copy.wait_recv()
            prev_copy.wait()
            form(0)
        if unit + 2 == units:
            finish(0)
    form(1)
    finish(1)

    for copy in s1 + s2 + g1 + g2 + g3 + zs + [w_copy]:
        copy.wait_send()
    for d in range(nz):
        to = 2 * ((zhi + d) % nz) + y // 2

        @pl.when(to != row)
        def _():
            remote(own.at[row], own.at[row], x_send.at[d], x_recv.at[0], (to, col)).wait_send()

    for i in range(nrow):
        here = tab.at[i, 0]
        remote(here, here, y_send.at[0, i], mate_recv.at[i], mate).wait_send()

        @pl.when(owner)
        def _():
            remote(here, here, y_send.at[1, i], outer_recv.at[i], outer).wait_send()

    for h in range(2):
        remote(away.at[h], back.at[h], p_send.at[h], p_recv.at[h], sibling).wait_send()
    for i in range(nrow):
        for par in range(2):
            for which in (core, 1 - core):
                out_copy(i, par, which).wait()


def local(nrow, ncol, sample_values, sample_codes, basis_tables, model_params, gram_prev, rhs_prev):
    ncell, width = basis_tables.shape[1:]
    lanes = 2 * ncell // nrow
    nz = ncol // 8
    tiles = sample_values.shape[1]
    tile = nrow * ncol
    total = tile * tiles
    piece = width // nrow
    dma = pltpu.SemaphoreType.DMA
    vmem = pl.BlockSpec(memory_space=pltpu.VMEM)
    anywhere = pl.BlockSpec(memory_space=pl.ANY)
    f32, bf16 = jnp.float32, jnp.bfloat16
    return pl.pallas_call(
        functools.partial(kernel, nrow, ncol),
        out_shape=(
            jax.ShapeDtypeStruct(gram_prev.shape, f32),
            jax.ShapeDtypeStruct(rhs_prev.shape, f32),
        ),
        in_specs=[vmem, vmem, vmem, vmem, anywhere, vmem],
        out_specs=(anywhere, vmem),
        scratch_shapes=[
            pltpu.VMEM((nrow, 2 * piece, ncell), bf16),
            pltpu.VMEM((nrow, 2, 2 * piece, ncell), bf16),
            pltpu.VMEM((nz, 2 * piece, ncell), bf16),
            pltpu.VMEM((nrow, MAXDEG, lanes), f32),
            pltpu.VMEM((8, MAXDEG, lanes), f32),
            pltpu.VMEM((MAXDEG, lanes), f32),
            pltpu.VMEM((nz, MAXDEG, lanes), f32),
            pltpu.VMEM((nrow, MAXDEG, lanes), f32),
            pltpu.VMEM((nrow, 1, 128), f32),
            pltpu.VMEM((ncol, nrow, 128), f32),
            pltpu.VMEM((128, tile), f32),
            pltpu.VMEM((2, 3 * MAXDEG, ncell), bf16),
            pltpu.VMEM((2, tiles, MAXDEG + piece, tile), f32),
            pltpu.VMEM((tiles, ncell, tile), bf16),
            pltpu.VMEM((tiles, tile), f32),
            pltpu.VMEM((2 * width + SIDE, total), bf16),
            pltpu.VMEM((2, width, total), bf16),
            pltpu.VMEM(gram_prev.shape, f32),
            pltpu.VMEM((2, width, width), f32),
            pltpu.VMEM((2, width, width), f32),
            dma((nrow,)), dma((nrow,)), dma((ncol,)), dma((ncol,)),
            dma((8,)), dma((8,)), dma((nz,)), dma((nz,)), dma((nrow,)), dma((nrow,)),
            dma((nz,)), dma((nz,)), dma((nz,)), dma((nrow,)), dma((2, nrow)), dma((nrow,)), dma((nrow,)),
            dma, dma, dma((2,)), dma((2,)), dma, dma((nrow, 2, 2)),
        ],
        compiler_params=pltpu.CompilerParams(
            collective_id=0, has_side_effects=True, vmem_limit_bytes=VMEM_LIMIT
        ),
    )(basis_tables, model_params, sample_values, sample_codes, gram_prev, rhs_prev)


def solution(mesh):
    placed = (
        P(None, ("row", "col")),
        P(None, ("row", "col")),
        P(None, None, "col"),
        P("col"),
        P("row", "col"),
        P("col"),
    )
    return jax.shard_map(
        functools.partial(local, mesh.shape["row"], mesh.shape["col"]),
        mesh=mesh,
        in_specs=placed,
        out_specs=(P("row", "col"), P("col")),
        check_vma=False,
    )
```

time: 1130 us -> 82.9 us (0.07)
  the two profiles are of different devices: /device:TPU:17 before, /device:TPU:37 now
where the time goes in v2:
time: 82.9 us; the launch traced here: 82.7 us
  Pallas kernels  78.3 us (94%)
  local copies, waits for them, and re-layouts  3.81 us (5%)
    pallas_call x1, Pallas kernels, local(): pl.pallas_call(functools.partial(kernel, nrow, ncol), out_shape=(jax.Shap...  78.3 us
    unnamed x4, local copies, waits for them, and re-layouts  3.81 us

profile of v2, /device:TPU:37, one launch (start us, length us, event | category | flops | bytes accessed | tf_op | source)
XLA Modules:
  0.0 82.7 jit_solution(1936097822514614406)
XLA Ops:
  0.6 78.3 %shard_map.77 = (f32[1536,384]{1,0:T(8,128)}, f32[384]{0:T(512)}) custom-call(bf16[2,512,384]{2,1,0:T(8,128)(2,1)} %basis_ref.1, f32[384]{0:T(512)} %params_ref.1, f32[4,16]{1,0:T(4,128)} %values_ref.1, s32[2,16]{1,0:T(2,128)} %codes_ref.1, f32[1536,384]{1,0:T(8,128)} %prev_ref.1, f32[384]{0:T(512)} %rhs_prev_ref.1), custom_call_target="tpu_custom_call" | custom-call | tf_op jit(solution)/shard_map/pallas_call | solution.py:378
  78.9 0.0 copy-start
  78.9 3.2 %copy.10 = f32[1536,384]{1,0:T(8,128)} copy(f32[1536,384]{1,0:T(8,128)} %get-tuple-element.4) | data formatting | bytes 4718592
  82.1 0.0 copy-done
  82.2 0.6 copy.11
Async XLA Ops:
  78.9 3.2 %copy-start = (f32[384]{0:T(512)S(1)}, f32[384]{0:T(512)}, u32[]{:S(2)}) copy-start(f32[384]{0:T(512)} %get-tuple-element.5) | copy-start | bytes 4612

commit v3 on v2

v3 whole, which is shorter than its diff:
```python
import functools
import math

import jax
import jax.numpy as jnp
from jax import lax
from jax.experimental import pallas as pl
from jax.experimental.pallas import tpu as pltpu
from jax.sharding import PartitionSpec as P

MAXDEG = 64
MESH = pl.DeviceIdType.MESH
VMEM_LIMIT = 52 * 1024 * 1024
NT = (((1,), (1,)), ((), ()))
SIDE = 16
PIECES = 8


def kernel(
    nrow, ncol,
    basis_ref, params_ref, values_ref, codes_ref, prev_ref, rhs_prev_ref,
    gram_ref, rhs_ref,
    own, tab, zbuf, part, land1, tot1, land2, sums, slots, samples,
    turned, pieces, grown, hots, pred, design, weighted, away, back,
    s1_send, s1_recv, s2_send, s2_recv,
    g1_send, g1_recv, g2_send, g2_recv, g3_send, g3_recv,
    z_send, z_recv, x_send, x_recv, y_send, y_recv,
    w_send, w_recv, p_send, p_recv, prev_sem,
):
    f32, bf16 = jnp.float32, jnp.bfloat16
    nz = ncol // 8
    row, col = lax.axis_index("row"), lax.axis_index("col")
    x, zlo = row // 2, row % 2
    zhi, yk = col // 8, col % 8
    y, core = yk // 2, yk % 2
    ncell, width = basis_ref.shape[1:]
    lanes = sums.shape[2]
    piece = width // PIECES
    share = PIECES // nrow
    tiles = values_ref.shape[1]
    tile = nrow * ncol
    total = tiles * tile
    scale = 1.0 / math.sqrt(total)

    def remote(src, dst, ssem, rsem, device):
        return pltpu.make_async_remote_copy(
            src_ref=src, dst_ref=dst, send_sem=ssem, recv_sem=rsem, device_id=device, device_id_type=MESH
        )

    left = (row, zhi * 8 + 2 * ((y + 3) % 4) + core)
    right = (row, zhi * 8 + 2 * ((y + 1) % 4) + core)
    sibling = (row, zhi * 8 + 2 * y + 1 - core)
    col_peers = [(row, (col + d) % ncol) for d in range(ncol)]
    row_peers = [((row + d) % nrow, col) for d in range(nrow)]
    near = [(row, zhi * 8 + (yk + d) % 8) for d in range(8)]
    far = [(row, ((zhi + d) % nz) * 8 + yk) for d in range(nz)]
    other = row + 1 - 2 * zlo
    hand = [(other, far[d][1]) if 2 * d == nz else far[d] for d in range(nz)]
    handed = [other if 2 * d == nz else row for d in range(nz)]
    parity = y % 2
    blocks = [(par, e) for par in range(2) for e in range(2)]
    offsets = (0, 3, 1, 2)

    barrier = pltpu.get_barrier_semaphore()
    greeted = col_peers[1:] + row_peers[1:] + [hand[d] for d in range(1, nz) if 2 * d == nz]
    for peer in greeted:
        pl.semaphore_signal(barrier, inc=1, device_id=peer, device_id_type=MESH)

    selves = 0
    for par, e in blocks:
        giver = (2 * y + e) // share
        if nz > 1:
            giver = jnp.where(2 * ((x - zhi + nz) % nz) == nz, giver + 1 - 2 * (giver % 2), giver)
        place = zhi * 8 + 2 * (2 * zlo + par) + core
        to_self = (giver == row) & (place == col)
        selves = selves + to_self.astype(jnp.int32)

        @pl.when(jnp.logical_not(to_self))
        def _():
            pl.semaphore_signal(barrier, inc=1, device_id=(giver, place), device_id_type=MESH)

    prev_copy = pltpu.make_async_copy(prev_ref, gram_ref, prev_sem)
    prev_copy.start()

    slots[row] = jnp.concatenate(
        [values_ref[i : i + 1, :] for i in range(4)]
        + [codes_ref[i : i + 1, :].astype(f32) for i in range(2)]
        + [jnp.zeros((1, 128 - 6 * tiles), f32)],
        axis=1,
    )
    for a in range(2):
        whole = jnp.concatenate(
            [basis_ref[a, :, 128 * j : 128 * (j + 1)].astype(f32).T for j in range(width // 128)], axis=0
        ).astype(bf16)
        for p in range(PIECES):
            own[p, a] = whole[piece * p : piece * (p + 1)]

    pl.semaphore_wait(barrier, len(greeted) + len(blocks) - selves)

    s1 = [remote(slots.at[row], slots.at[row], s1_send.at[d], s1_recv.at[d], row_peers[d]) for d in range(1, nrow)]
    for copy in s1:
        copy.start()

    def pass_z(d, u):
        return [
            remote(own.at[row * share + m, u], zbuf.at[nz - d, m, u], z_send.at[d, m, u], z_recv.at[nz - d, m, u], hand[d])
            for m in range(share)
        ]

    def pass_x(d, u):
        to = 2 * ((zhi + d) % nz) + y // 2
        for m in range(share):
            p = handed[d] * share + m
            target = zhi * 8 + 2 * (p // 2) + core
            source = own.at[p, u] if d == 0 else zbuf.at[d, m, u]
            place = tab.at[0, parity, p % 2, u]
            arrived = x_recv.at[parity, p % 2, u]
            to_self = (to == row) & (target == col)

            @pl.when(jnp.logical_not(to_self))
            def _():
                remote(source, place, x_send.at[d, m, u], arrived, (to, target)).start()

            @pl.when(to_self)
            def _():
                pltpu.make_async_copy(source, place, arrived).start()

    zs = []
    for u in range(2):
        for d in range(1, nz):
            zs += pass_z(d, u)
    for copy in zs:
        copy.start()
    for u in range(2):
        pass_x(0, u)

    params = params_ref[...].reshape(1, width)
    per = ncell // lanes
    for a in range(2):
        amount = None
        for j in range(width // 128):
            term = basis_ref[a, :, 128 * j : 128 * (j + 1)].astype(f32) * params[:, 128 * j : 128 * (j + 1)]
            amount = term if amount is None else amount + term
        amount = amount.T
        amount = amount[:MAXDEG] + amount[MAXDEG:]
        for i in range(per):
            part[a * per + i] = amount[:, i * lanes : (i + 1) * lanes]
    g1 = [remote(part.at[row], land1.at[d], g1_send.at[d], g1_recv.at[d], near[d]) for d in range(1, 8)]
    for copy in g1:
        copy.start()

    for copy in s1:
        copy.wait_recv()
    for i in range(nrow):
        samples[col, pl.ds(i, 1)] = slots[i]
    s2 = [
        remote(samples.at[col], samples.at[col], s2_send.at[d], s2_recv.at[d], col_peers[d]) for d in range(1, ncol)
    ]
    for copy in s2:
        copy.start()

    for u in range(2):
        for d in range(1, nz):
            for m in range(share):
                here = zbuf.at[d, m, u]
                remote(here, here, z_send.at[d, m, u], z_recv.at[d, m, u], hand[d]).wait_recv()
            pass_x(d, u)

    def pass_y(u):
        for par, e in blocks:
            here = tab.at[0, par, e, u]
            pltpu.make_async_copy(here, here, x_recv.at[par, e, u]).wait()
            remote(here, tab.at[1, par, e, u], y_send.at[0, par, e, u], y_recv.at[0, par, e, u], right).start()
            remote(here, tab.at[2, par, e, u], y_send.at[1, par, e, u], y_recv.at[1, par, e, u], left).start()

    def arrive(g, par, e, u):
        here = tab.at[g, par, e, u]
        remote(here, here, y_send.at[0, par, e, u], y_recv.at[g - 1, par, e, u], right).wait_recv()

    def pass_on(u):
        for par in range(2):
            for g, to in ((1, right), (2, left)):
                e = g - 1
                arrive(g, par, e, u)
                remote(
                    tab.at[g, par, e, u], tab.at[3, par, e, u], y_send.at[2, par, e, u], y_recv.at[2, par, e, u], to
                ).start()

    def field(number, k):
        return turned[pl.ds(number * tiles + k, 1), :]

    def span(k):
        return pl.ds(pl.multiple_of(k * tile, tile), tile)

    exponent = (lax.broadcasted_iota(jnp.int32, (MAXDEG, tile), 0) + 1).astype(f32)
    cells = lax.broadcasted_iota(jnp.int32, (ncell, tile), 0).astype(jnp.int16)
    reach = grown.shape[2]

    def build_own(k, carry):
        hot = jnp.where(cells == field(4, k).astype(jnp.int32).astype(jnp.int16), jnp.bfloat16(1), jnp.bfloat16(0))
        hots[k] = hot
        grow = jnp.exp(field(2, k) * exponent)
        grows = []
        for a in range(2):
            value = grow * field(a, k)
            value = jnp.concatenate([value, value], axis=0)
            grown[a, k] = value[:reach]
            grows.append(value)
        picked = jnp.dot(own[...].reshape(2 * width, ncell), hot, preferred_element_type=f32)
        for p in range(PIECES):
            first = 2 * piece * p
            at = (p * piece) % MAXDEG
            weighted[0, p * piece : (p + 1) * piece, span(k)] = (
                picked[first : first + piece] * grows[0][at : at + piece]
                + picked[first + piece : first + 2 * piece] * grows[1][at : at + piece]
            ).astype(bf16)
        return carry

    def mixed(picked, k, p):
        at = pl.ds(pl.multiple_of((p * piece) % MAXDEG, 16), piece)
        return (picked[:piece] * grown[0, k, at] + picked[piece:] * grown[1, k, at]).astype(bf16)

    def predict(picked, k):
        value = None
        for a in range(2):
            three = picked[3 * MAXDEG * a : 3 * MAXDEG * (a + 1)]
            term = grown[a, k, :MAXDEG] * (three[:MAXDEG] + three[MAXDEG : 2 * MAXDEG] + three[2 * MAXDEG :])
            value = term if value is None else value + term
        pred[pl.ds(k, 1), :] = jnp.sum(value, axis=0, keepdims=True)

    def weigh(k, carry):
        weighted[0, :, span(k)] = (weighted[0, :, span(k)].astype(f32) * field(5, k)).astype(bf16)
        rest = field(3, k)
        split = []
        for n in range(3):
            split.append(rest.astype(bf16).astype(f32))
            rest = rest - split[-1]
        split.append(jnp.zeros((SIDE - 3, tile), f32))
        design[width : width + SIDE, span(k)] = jnp.concatenate(split, axis=0).astype(bf16)
        return carry

    def origin(g, e):
        return 2 * ((y + offsets[g]) % 4) + e

    def build_rows(g):
        def body(k, carry):
            lhs = tab[g].reshape(8 * piece, ncell)
            if g == 0:
                lhs = jnp.concatenate([lhs, pieces[...].reshape(6 * MAXDEG, ncell)], axis=0)
            picked = jnp.dot(lhs, hots[k], preferred_element_type=f32)
            if g == 0:
                predict(picked[8 * piece :], k)
            for n, (par, e) in enumerate(blocks):
                at = (4 * g + n) * piece + (SIDE if g >= 2 else 0)
                design[at : at + piece, span(k)] = mixed(picked[2 * piece * n : 2 * piece * (n + 1)], k, origin(g, e))
            return carry

        lax.fori_loop(0, tiles, body, 0, unroll=4)

    def collect(h, which, product):
        for n in range(8):
            par, e = blocks[n % 4]
            first = (2 * par + which) * width + origin(2 * h + n // 4, e) * piece
            at = pl.ds(pl.multiple_of(first, 16), piece)
            gram_ref[at, :] = gram_ref[at, :] + scale * product[n * piece : (n + 1) * piece]

    def swap(h):
        return remote(away.at[h], back.at[h], p_send.at[h], p_recv.at[h], sibling)

    def form(h):
        rows = width + (SIDE if h == 0 else 0)
        first = 0 if h == 0 else width + SIDE
        both = weighted[...].reshape(2 * width, total)
        product = lax.dot_general(design[first : first + rows], both, NT, preferred_element_type=f32)
        away[h] = product[:width, width:]
        swap(h).start()
        collect(h, core, product[:width, :width])
        if h == 0:
            rhs_ref[...] = rhs_prev_ref[...] + scale * jnp.sum(product[width : width + 8, :width], axis=0)

    def finish(h):
        swap(h).wait_recv()
        collect(h, 1 - core, back[h])

    def some(body, number, parts):
        lax.fori_loop(number * tiles // parts, (number + 1) * tiles // parts, body, 0, unroll=4)

    for copy in g1:
        copy.wait_recv()
    amount = part[row]
    for d in range(1, 8):
        amount = amount + land1[d]
    tot1[...] = amount
    g2 = [remote(tot1, land2.at[d], g2_send.at[d], g2_recv.at[d], far[d]) for d in range(1, nz)]
    for copy in g2:
        copy.start()

    for copy in s2:
        copy.wait_recv()
    turned[...] = samples[...].reshape(tile, 128).T
    for n in range(4):
        some(build_own, n, 4)
        if n == 1:
            for copy in g2:
                copy.wait_recv()
            amount = tot1[...]
            for d in range(1, nz):
                amount = amount + land2[d]
            sums[row] = amount
            g3 = [
                remote(sums.at[row], sums.at[row], g3_send.at[d], g3_recv.at[d], row_peers[d])
                for d in range(1, nrow)
            ]
            for copy in g3:
                copy.start()
        if n == 2:
            pass_y(0)
    pass_y(1)

    for copy in g3:
        copy.wait_recv()
    for a in range(2):
        for i in range(per):
            value = sums[a * per + i]
            for n in range(3):
                part_value = value.astype(bf16)
                pieces[a, n * MAXDEG : (n + 1) * MAXDEG, i * lanes : (i + 1) * lanes] = part_value
                value = value - part_value.astype(f32)
    build_rows(0)
    pass_on(0)

    residual = turned[3 * tiles : 4 * tiles, :] - pred[...]
    group = turned[5 * tiles : 6 * tiles, :]
    size = jnp.abs(residual)
    limit = jnp.zeros_like(size)
    for number in range(2):
        hot = (group == float(number)).astype(f32)
        count = jnp.sum(jnp.sum(hot, axis=0, keepdims=True), axis=1, keepdims=True)
        spread = jnp.sum(jnp.sum(hot * size, axis=0, keepdims=True), axis=1, keepdims=True)
        limit = limit + hot * (1.345 * spread / jnp.maximum(count, 1.0))
    turned[3 * tiles : 4 * tiles, :] = residual
    turned[5 * tiles : 6 * tiles, :] = limit / jnp.maximum(size, limit)
    some(weigh, 0, 1)
    w_copy = remote(weighted.at[0], weighted.at[1], w_send, w_recv, sibling)
    w_copy.start()

    pass_on(1)
    for par in range(2):
        for u in range(2):
            arrive(1, par, 1, u)
    build_rows(1)
    for par in range(2):
        for u in range(2):
            arrive(2, par, 0, u)
    build_rows(2)
    w_copy.wait_recv()
    prev_copy.wait()
    form(0)
    for par, e in blocks:
        for u in range(2):
            arrive(3, par, e, u)
    build_rows(3)
    finish(0)
    form(1)
    finish(1)

    for copy in s1 + s2 + g1 + g2 + g3 + zs + [w_copy]:
        copy.wait_send()
    for u in range(2):
        for d in range(nz):
            to = 2 * ((zhi + d) % nz) + y // 2
            for m in range(share):
                p = handed[d] * share + m
                target = zhi * 8 + 2 * (p // 2) + core

                @pl.when((to != row) | (target != col))
                def _():
                    here = own.at[p, u]
                    remote(here, here, x_send.at[d, m, u], x_recv.at[0, 0, u], (to, target)).wait_send()

        for par, e in blocks:
            for n in range(3):
                here = tab.at[n, par, e, u]
                remote(here, here, y_send.at[n, par, e, u], y_recv.at[0, par, e, u], right).wait_send()
    for h in range(2):
        swap(h).wait_send()


def local(nrow, ncol, sample_values, sample_codes, basis_tables, model_params, gram_prev, rhs_prev):
    ncell, width = basis_tables.shape[1:]
    lanes = 2 * ncell // nrow
    nz = ncol // 8
    tiles = sample_values.shape[1]
    tile = nrow * ncol
    total = tile * tiles
    piece = width // PIECES
    dma = pltpu.SemaphoreType.DMA
    vmem = pl.BlockSpec(memory_space=pltpu.VMEM)
    anywhere = pl.BlockSpec(memory_space=pl.ANY)
    f32, bf16 = jnp.float32, jnp.bfloat16
    return pl.pallas_call(
        functools.partial(kernel, nrow, ncol),
        out_shape=(
            pltpu.VMEM(gram_prev.shape, f32),
            pltpu.VMEM(rhs_prev.shape, f32),
        ),
        in_specs=[vmem, vmem, vmem, vmem, anywhere, vmem],
        out_specs=(vmem, vmem),
        scratch_shapes=[
            pltpu.VMEM((PIECES, 2, piece, ncell), bf16),
            pltpu.VMEM((4, 2, 2, 2, piece, ncell), bf16),
            pltpu.VMEM((nz, PIECES // nrow, 2, piece, ncell), bf16),
            pltpu.VMEM((nrow, MAXDEG, lanes), f32),
            pltpu.VMEM((8, MAXDEG, lanes), f32),
            pltpu.VMEM((MAXDEG, lanes), f32),
            pltpu.VMEM((nz, MAXDEG, lanes), f32),
            pltpu.VMEM((nrow, MAXDEG, lanes), f32),
            pltpu.VMEM((nrow, 1, 128), f32),
            pltpu.VMEM((ncol, nrow, 128), f32),
            pltpu.VMEM((128, tile), f32),
            pltpu.VMEM((2, 3 * MAXDEG, ncell), bf16),
            pltpu.VMEM((2, tiles, MAXDEG + piece, tile), f32),
            pltpu.VMEM((tiles, ncell, tile), bf16),
            pltpu.VMEM((tiles, tile), f32),
            pltpu.VMEM((2 * width + SIDE, total), bf16),
            pltpu.VMEM((2, width, total), bf16),
            pltpu.VMEM((2, width, width), f32),
            pltpu.VMEM((2, width, width), f32),
            dma((nrow,)), dma((nrow,)), dma((ncol,)), dma((ncol,)),
            dma((8,)), dma((8,)), dma((nz,)), dma((nz,)), dma((nrow,)), dma((nrow,)),
            dma((nz, PIECES // nrow, 2)), dma((nz, PIECES // nrow, 2)), dma((nz, PIECES // nrow, 2)),
            dma((2, 2, 2)), dma((3, 2, 2, 2)), dma((3, 2, 2, 2)),
            dma, dma, dma((2,)), dma((2,)), dma,
        ],
        compiler_params=pltpu.CompilerParams(
            collective_id=0, has_side_effects=True, vmem_limit_bytes=VMEM_LIMIT
        ),
    )(basis_tables, model_params, sample_values, sample_codes, gram_prev, rhs_prev)


def solution(mesh):
    placed = (
        P(None, ("row", "col")),
        P(None, ("row", "col")),
        P(None, None, "col"),
        P("col"),
        P("row", "col"),
        P("col"),
    )
    return jax.shard_map(
        functools.partial(local, mesh.shape["row"], mesh.shape["col"]),
        mesh=mesh,
        in_specs=placed,
        out_specs=(P("row", "col"), P("col")),
        check_vma=False,
    )
```

time: 82.9 us -> 66.1 us (0.80)
  the two profiles are of different devices: /device:TPU:37 before, /device:TPU:1 now
where the time goes in v3:
time: 66.1 us; the launch traced here: 66 us
  Pallas kernels  63.4 us (96%)
  local copies, waits for them, and re-layouts  1.99 us (3%)
    pallas_call x1, Pallas kernels, local(): pl.pallas_call(functools.partial(kernel, nrow, ncol), out_shape=(pltpu.VM...  63.4 us
    unnamed x2, local copies, waits for them, and re-layouts  1.99 us

profile of v3, /device:TPU:1, one launch (start us, length us, event | category | flops | bytes accessed | tf_op | source)
XLA Modules:
  0.0 66.0 jit_solution(11960023767477477075)
XLA Ops:
  0.6 63.4 %shard_map.77 = (f32[1536,384]{1,0:T(8,128)S(1)}, f32[384]{0:T(512)S(1)}) custom-call(bf16[2,512,384]{2,1,0:T(8,128)(2,1)} %basis_ref.1, f32[384]{0:T(512)} %params_ref.1, f32[4,16]{1,0:T(4,128)} %values_ref.1, s32[2,16]{1,0:T(2,128)} %codes_ref.1, f32[1536,384]{1,0:T(8,128)} %prev_ref.1, f32[384]{0:T(512)} %rhs_prev_ref.1), custom_call_target="tpu_custom_call" | custom-call | tf_op jit(solution)/shard_map/pallas_call | solution.py:401
  64.0 1.4 %copy.10 = f32[1536,384]{1,0:T(8,128)} copy(f32[1536,384]{1,0:T(8,128)S(1)} %get-tuple-element.2) | data formatting | bytes 4718592
  65.4 0.6 copy.11

commit v4 on v3

v4 whole, which is shorter than its diff:
```python
import functools
import math

import jax
import jax.numpy as jnp
from jax import lax
from jax.experimental import pallas as pl
from jax.experimental.pallas import tpu as pltpu
from jax.sharding import PartitionSpec as P

MAXDEG = 64
MESH = pl.DeviceIdType.MESH
VMEM_LIMIT = 52 * 1024 * 1024
NT = (((1,), (1,)), ((), ()))
SIDE = 16
PARTS = ((0, 32), (32, 16))
PIECES = 8
UNROLL = 4


def kernel(
    nrow, ncol,
    basis_ref, params_ref, values_ref, codes_ref, prev_ref, rhs_prev_ref,
    gram_ref, rhs_ref,
    own, tab, zbuf, part, land1, tot1, land2, sums, slots, samples,
    turned, grown, hots, design, weighted, away, back,
    s1_send, s1_recv, s2_send, s2_recv,
    g1_send, g1_recv, g2_send, g2_recv, g3_send, g3_recv,
    z_send, z_recv, x_send, x_recv, y_send, y_recv,
    w_send, w_recv, p_send, p_recv, prev_sem,
):
    f32, bf16 = jnp.float32, jnp.bfloat16
    nz = ncol // 8
    row, col = lax.axis_index("row"), lax.axis_index("col")
    x, zlo = row // 2, row % 2
    zhi, yk = col // 8, col % 8
    y, core = yk // 2, yk % 2
    ncell, width = basis_ref.shape[1:]
    piece = width // PIECES
    share = PIECES // nrow
    quarter = 4 * piece
    tiles = values_ref.shape[1]
    tile = nrow * ncol
    total = tiles * tile
    mine = tiles // nrow
    scale = 1.0 / math.sqrt(total)

    def remote(src, dst, ssem, rsem, device):
        return pltpu.make_async_remote_copy(
            src_ref=src, dst_ref=dst, send_sem=ssem, recv_sem=rsem, device_id=device, device_id_type=MESH
        )

    left = (row, zhi * 8 + 2 * ((y + 3) % 4) + core)
    right = (row, zhi * 8 + 2 * ((y + 1) % 4) + core)
    sibling = (row, zhi * 8 + 2 * y + 1 - core)
    col_peers = [(row, (col + d) % ncol) for d in range(ncol)]
    row_peers = [((row + d) % nrow, col) for d in range(nrow)]
    near = [(row, zhi * 8 + (yk + d) % 8) for d in range(8)]
    far = [(row, ((zhi + d) % nz) * 8 + yk) for d in range(nz)]
    other = row + 1 - 2 * zlo
    hand = [(other, far[d][1]) if 2 * d == nz else far[d] for d in range(nz)]
    handed = [other if 2 * d == nz else row for d in range(nz)]
    parity = y % 2
    blocks = [(par, e) for par in range(2) for e in range(2)]
    offsets = (0, 3, 1, 2)

    barrier = pltpu.get_barrier_semaphore()
    greeted = col_peers[1:] + row_peers[1:] + [hand[d] for d in range(1, nz) if 2 * d == nz]
    for peer in greeted:
        pl.semaphore_signal(barrier, inc=1, device_id=peer, device_id_type=MESH)

    selves = 0
    for par, e in blocks:
        giver = (2 * y + e) // share
        if nz > 1:
            giver = jnp.where(2 * ((x - zhi + nz) % nz) == nz, giver + 1 - 2 * (giver % 2), giver)
        place = zhi * 8 + 2 * (2 * zlo + par) + core
        to_self = (giver == row) & (place == col)
        selves = selves + to_self.astype(jnp.int32)

        @pl.when(jnp.logical_not(to_self))
        def _():
            pl.semaphore_signal(barrier, inc=1, device_id=(giver, place), device_id_type=MESH)

    prev_copy = pltpu.make_async_copy(prev_ref, gram_ref, prev_sem)
    prev_copy.start()

    slots[row] = jnp.concatenate(
        [values_ref[i : i + 1, :] for i in range(4)]
        + [codes_ref[i : i + 1, :].astype(f32) for i in range(2)]
        + [jnp.zeros((1, 128 - 6 * tiles), f32)],
        axis=1,
    )
    for a in range(2):
        whole = jnp.concatenate(
            [basis_ref[a, :, 128 * j : 128 * (j + 1)].astype(f32).T for j in range(width // 128)], axis=0
        ).astype(bf16)
        for p in range(PIECES):
            for begin, rows in PARTS:
                own[p, 2 * begin + a * rows : 2 * begin + (a + 1) * rows] = whole[
                    piece * p + begin : piece * p + begin + rows
                ]

    pl.semaphore_wait(barrier, len(greeted) + len(blocks) - selves)

    s1 = [remote(slots.at[row], slots.at[row], s1_send.at[d], s1_recv.at[d], row_peers[d]) for d in range(1, nrow)]
    for copy in s1:
        copy.start()

    def half(ref, u):
        begin, rows = PARTS[u]
        return ref.at[pl.ds(2 * begin, 2 * rows)]

    def pass_z(d, u):
        return [
            remote(half(own.at[row * share + m], u), half(zbuf.at[nz - d, m], u), z_send.at[d, m, u], z_recv.at[nz - d, m, u], hand[d])
            for m in range(share)
        ]

    def pass_x(d, u):
        to = 2 * ((zhi + d) % nz) + y // 2
        for m in range(share):
            p = handed[d] * share + m
            target = zhi * 8 + 2 * (p // 2) + core
            source = half(own.at[p] if d == 0 else zbuf.at[d, m], u)
            place = half(tab.at[0, parity, p % 2], u)
            arrived = x_recv.at[parity, p % 2, u]
            to_self = (to == row) & (target == col)

            @pl.when(jnp.logical_not(to_self))
            def _():
                remote(source, place, x_send.at[d, m, u], arrived, (to, target)).start()

            @pl.when(to_self)
            def _():
                pltpu.make_async_copy(source, place, arrived).start()

    zs = [[copy for d in range(1, nz) for copy in pass_z(d, u)] for u in range(2)]
    for copy in zs[0]:
        copy.start()
    for u in range(2):
        pass_x(0, u)

    rest = params_ref[...].reshape(1, width)
    terms = []
    for n in range(3):
        terms.append(rest.astype(bf16).astype(f32))
        rest = rest - terms[-1]
    terms = jnp.concatenate(terms + [jnp.zeros((SIDE - 3, width), f32)], axis=0).astype(bf16)

    for copy in s1:
        copy.wait_recv()
    for i in range(nrow):
        samples[col, pl.ds(i, 1)] = slots[i]
    s2 = [
        remote(samples.at[col], samples.at[col], s2_send.at[d], s2_recv.at[d], col_peers[d]) for d in range(1, ncol)
    ]
    for copy in s2:
        copy.start()
    for copy in zs[1]:
        copy.start()

    def pass_zx(u):
        for d in range(1, nz):
            for m in range(share):
                here = half(zbuf.at[d, m], u)
                remote(here, here, z_send.at[d, m, u], z_recv.at[d, m, u], hand[d]).wait_recv()
            pass_x(d, u)

    def pass_y(u):
        for par, e in blocks:
            here = half(tab.at[0, par, e], u)
            pltpu.make_async_copy(here, here, x_recv.at[par, e, u]).wait()
            remote(here, half(tab.at[1, par, e], u), y_send.at[0, par, e, u], y_recv.at[0, par, e, u], right).start()
            remote(here, half(tab.at[2, par, e], u), y_send.at[1, par, e, u], y_recv.at[1, par, e, u], left).start()

    def arrive(g, par, e, u):
        here = half(tab.at[g, par, e], u)
        remote(here, here, y_send.at[0, par, e, u], y_recv.at[g - 1, par, e, u], right).wait_recv()

    def pass_on(u):
        for par in range(2):
            for g, to in ((1, right), (2, left)):
                e = g - 1
                arrive(g, par, e, u)
                remote(
                    half(tab.at[g, par, e], u), half(tab.at[3, par, e], u), y_send.at[2, par, e, u], y_recv.at[2, par, e, u], to
                ).start()

    def field(number, k):
        return turned[pl.ds(number * tiles + k, 1), :]

    def span(k):
        return pl.ds(pl.multiple_of(k * tile, tile), tile)

    exponent = (lax.broadcasted_iota(jnp.int32, (MAXDEG, tile), 0) + 1).astype(f32)
    cells = lax.broadcasted_iota(jnp.int32, (ncell, tile), 0).astype(jnp.int16)
    reach = grown.shape[2]

    def build_own(number, carry):
        k = (number + row * mine) % tiles
        hot = jnp.where(cells == field(4, k).astype(jnp.int32).astype(jnp.int16), jnp.bfloat16(1), jnp.bfloat16(0))
        hots[k] = hot
        grow = jnp.exp(field(2, k) * exponent)
        grows = []
        for a in range(2):
            value = grow * field(a, k)
            value = jnp.concatenate([value, value], axis=0)
            grown[a, k] = value[:reach]
            grows.append(value)
        picked = jnp.dot(own[...].reshape(2 * width, ncell), hot, preferred_element_type=f32)
        for p in range(PIECES):
            for begin, rows in PARTS:
                first = 2 * (piece * p + begin)
                at = (p * piece + begin) % MAXDEG
                weighted[0, p * piece + begin : p * piece + begin + rows, span(k)] = (
                    picked[first : first + rows] * grows[0][at : at + rows]
                    + picked[first + rows : first + 2 * rows] * grows[1][at : at + rows]
                ).astype(bf16)
        return carry

    def mixed(picked, k, begin, rows):
        at = pl.ds(pl.multiple_of(begin % MAXDEG, 16), rows)
        return (picked[:rows] * grown[0, k, at] + picked[rows:] * grown[1, k, at]).astype(bf16)

    def weigh(k, carry):
        weighted[0, :, span(k)] = (weighted[0, :, span(k)].astype(f32) * field(5, k)).astype(bf16)
        rest = field(3, k)
        split = []
        for n in range(3):
            split.append(rest.astype(bf16).astype(f32))
            rest = rest - split[-1]
        split.append(jnp.zeros((SIDE - 3, tile), f32))
        design[3 * quarter : 3 * quarter + SIDE, span(k)] = jnp.concatenate(split, axis=0).astype(bf16)
        return carry

    def origin(g, e):
        return 2 * ((y + offsets[g]) % 4) + e

    def first_row(g):
        return g * quarter + (SIDE if g > 2 else 0)

    def build_rows(groups, parts):
        lo = PARTS[parts[0]][0]
        hi = sum(PARTS[parts[-1]])
        size = 2 * (hi - lo)

        def body(k, carry):
            lhs = tab[groups[0] : groups[-1] + 1, :, :, 2 * lo : 2 * hi].reshape(4 * size * len(groups), ncell)
            picked = jnp.dot(lhs, hots[k], preferred_element_type=f32)
            for j, g in enumerate(groups):
                for n, (par, e) in enumerate(blocks):
                    for u in parts:
                        begin, rows = PARTS[u]
                        at = first_row(g) + n * piece + begin
                        first = size * (4 * j + n) + 2 * (begin - lo)
                        design[at : at + rows, span(k)] = mixed(
                            picked[first : first + 2 * rows], k, origin(g, e) * piece + begin, rows
                        )
            return carry

        lax.fori_loop(0, tiles, body, 0, unroll=UNROLL)

    def collect(groups, which, product):
        for j, g in enumerate(groups):
            for n, (par, e) in enumerate(blocks):
                at = pl.ds(pl.multiple_of((2 * par + which) * width + origin(g, e) * piece, 16), piece)
                begin = j * quarter + n * piece
                gram_ref[at, :] = gram_ref[at, :] + scale * product[begin : begin + piece]

    def swap(groups):
        at, g = pl.ds(groups[0] * quarter, len(groups) * quarter), groups[0]
        return remote(away.at[at], back.at[at], p_send.at[g], p_recv.at[g], sibling)

    def form(groups):
        count = len(groups) * quarter
        rows = count + (SIDE if groups[0] == 0 else 0)
        first = first_row(groups[0])
        both = weighted[...].reshape(2 * width, total)
        product = lax.dot_general(design[first : first + rows], both, NT, preferred_element_type=f32)
        away[groups[0] * quarter : groups[0] * quarter + count] = product[:count, width:]
        swap(groups).start()
        collect(groups, core, product[:count, :width])
        if groups[0] == 0:
            rhs_ref[...] = rhs_prev_ref[...] + scale * jnp.sum(product[count : count + 8, :width], axis=0)

    def finish(groups):
        swap(groups).wait_recv()
        collect(groups, 1 - core, back[groups[0] * quarter : (groups[-1] + 1) * quarter])

    def some(body, number, parts):
        lax.fori_loop(number * tiles // parts, (number + 1) * tiles // parts, body, 0, unroll=UNROLL)

    pass_zx(0)
    for copy in s2:
        copy.wait_recv()
    turned[...] = samples[...].reshape(tile, 128).T
    some(build_own, 0, 4)
    early = -(-4 * mine // tiles)
    for n in range(1, early):
        some(build_own, n, 4)
    for j in range(mine):
        value = jnp.dot(terms, weighted[0, :, span(row * mine + j)], preferred_element_type=f32)
        part[j : j + 1, :] = jnp.sum(value[:8], axis=0, keepdims=True)
    g1 = [remote(part, land1.at[d], g1_send.at[d], g1_recv.at[d], near[d]) for d in range(1, 8)]
    for copy in g1:
        copy.start()
    for n in range(early, 2):
        some(build_own, n, 4)
    pass_zx(1)
    some(build_own, 2, 4)
    for copy in g1:
        copy.wait_recv()
    amount = part[...]
    for d in range(1, 8):
        amount = amount + land1[d]
    tot1[...] = amount
    g2 = [remote(tot1, land2.at[d], g2_send.at[d], g2_recv.at[d], far[d]) for d in range(1, nz)]
    for copy in g2:
        copy.start()
    some(build_own, 3, 4)
    pass_y(0)
    for copy in g2:
        copy.wait_recv()
    amount = tot1[...]
    for d in range(1, nz):
        amount = amount + land2[d]
    sums[row] = amount
    g3 = [remote(sums.at[row], sums.at[row], g3_send.at[d], g3_recv.at[d], row_peers[d]) for d in range(1, nrow)]
    for copy in g3:
        copy.start()
    pass_y(1)
    build_rows((0,), (0, 1))
    pass_on(0)
    for copy in g3:
        copy.wait_recv()

    residual = turned[3 * tiles : 4 * tiles, :] - jnp.concatenate([sums[r] for r in range(nrow)], axis=0)
    group = turned[5 * tiles : 6 * tiles, :]
    size = jnp.abs(residual)
    limit = jnp.zeros_like(size)
    for number in range(2):
        hot = (group == float(number)).astype(f32)
        count = jnp.sum(jnp.sum(hot, axis=0, keepdims=True), axis=1, keepdims=True)
        spread = jnp.sum(jnp.sum(hot * size, axis=0, keepdims=True), axis=1, keepdims=True)
        limit = limit + hot * (1.345 * spread / jnp.maximum(count, 1.0))
    turned[3 * tiles : 4 * tiles, :] = residual
    turned[5 * tiles : 6 * tiles, :] = limit / jnp.maximum(size, limit)
    some(weigh, 0, 1)
    w_copy = remote(weighted.at[0], weighted.at[1], w_send, w_recv, sibling)
    w_copy.start()

    for par in range(2):
        arrive(1, par, 1, 0)
        arrive(2, par, 0, 0)
    build_rows((1, 2), (0,))
    pass_on(1)
    for par in range(2):
        arrive(1, par, 1, 1)
        arrive(2, par, 0, 1)
    build_rows((1, 2), (1,))
    w_copy.wait_recv()
    prev_copy.wait()
    form((0, 1, 2))
    for par, e in blocks:
        for u in range(2):
            arrive(3, par, e, u)
    build_rows((3,), (0, 1))
    form((3,))
    finish((0, 1, 2))
    finish((3,))

    for copy in s1 + s2 + g1 + g2 + g3 + zs[0] + zs[1] + [w_copy]:
        copy.wait_send()
    for u in range(2):
        for d in range(nz):
            to = 2 * ((zhi + d) % nz) + y // 2
            for m in range(share):
                p = handed[d] * share + m
                target = zhi * 8 + 2 * (p // 2) + core

                @pl.when((to != row) | (target != col))
                def _():
                    here = half(own.at[p], u)
                    remote(here, here, x_send.at[d, m, u], x_recv.at[0, 0, u], (to, target)).wait_send()

        for par, e in blocks:
            for n in range(3):
                here = half(tab.at[n, par, e], u)
                remote(here, here, y_send.at[n, par, e, u], y_recv.at[0, par, e, u], right).wait_send()
    for groups in ((0, 1, 2), (3,)):
        swap(groups).wait_send()


def local(nrow, ncol, sample_values, sample_codes, basis_tables, model_params, gram_prev, rhs_prev):
    ncell, width = basis_tables.shape[1:]
    nz = ncol // 8
    tiles = sample_values.shape[1]
    tile = nrow * ncol
    total = tile * tiles
    piece = width // PIECES
    dma = pltpu.SemaphoreType.DMA
    vmem = pl.BlockSpec(memory_space=pltpu.VMEM)
    anywhere = pl.BlockSpec(memory_space=pl.ANY)
    f32, bf16 = jnp.float32, jnp.bfloat16
    return pl.pallas_call(
        functools.partial(kernel, nrow, ncol),
        out_shape=(
            pltpu.VMEM(gram_prev.shape, f32),
            pltpu.VMEM(rhs_prev.shape, f32),
        ),
        in_specs=[vmem, vmem, vmem, vmem, anywhere, vmem],
        out_specs=(vmem, vmem),
        scratch_shapes=[
            pltpu.VMEM((PIECES, 2 * piece, ncell), bf16),
            pltpu.VMEM((4, 2, 2, 2 * piece, ncell), bf16),
            pltpu.VMEM((nz, PIECES // nrow, 2 * piece, ncell), bf16),
            pltpu.VMEM((tiles // nrow, tile), f32),
            pltpu.VMEM((8, tiles // nrow, tile), f32),
            pltpu.VMEM((tiles // nrow, tile), f32),
            pltpu.VMEM((nz, tiles // nrow, tile), f32),
            pltpu.VMEM((nrow, tiles // nrow, tile), f32),
            pltpu.VMEM((nrow, 1, 128), f32),
            pltpu.VMEM((ncol, nrow, 128), f32),
            pltpu.VMEM((128, tile), f32),
            pltpu.VMEM((2, tiles, MAXDEG + piece, tile), f32),
            pltpu.VMEM((tiles, ncell, tile), bf16),
            pltpu.VMEM((2 * width + SIDE, total), bf16),
            pltpu.VMEM((2, width, total), bf16),
            pltpu.VMEM((2 * width, width), f32),
            pltpu.VMEM((2 * width, width), f32),
            dma((nrow,)), dma((nrow,)), dma((ncol,)), dma((ncol,)),
            dma((8,)), dma((8,)), dma((nz,)), dma((nz,)), dma((nrow,)), dma((nrow,)),
            dma((nz, PIECES // nrow, 2)), dma((nz, PIECES // nrow, 2)), dma((nz, PIECES // nrow, 2)),
            dma((2, 2, 2)), dma((3, 2, 2, 2)), dma((3, 2, 2, 2)),
            dma, dma, dma((4,)), dma((4,)), dma,
        ],
        compiler_params=pltpu.CompilerParams(
            collective_id=0, has_side_effects=True, vmem_limit_bytes=VMEM_LIMIT
        ),
    )(basis_tables, model_params, sample_values, sample_codes, gram_prev, rhs_prev)


def solution(mesh):
    placed = (
        P(None, ("row", "col")),
        P(None, ("row", "col")),
        P(None, None, "col"),
        P("col"),
        P("row", "col"),
        P("col"),
    )
    return jax.shard_map(
        functools.partial(local, mesh.shape["row"], mesh.shape["col"]),
        mesh=mesh,
        in_specs=placed,
        out_specs=(P("row", "col"), P("col")),
        check_vma=False,
    )
```

time: 66.1 us -> 63.4 us (0.959)
  the two profiles are of different devices: /device:TPU:1 before, /device:TPU:17 now
where the time goes in v4:
time: 63.4 us; the launch traced here: 63.3 us
  Pallas kernels  60.6 us (96%)
  local copies, waits for them, and re-layouts  1.99 us (3%)
  between operations  0.64 us (1%)
    pallas_call x1, Pallas kernels, local(): pl.pallas_call(functools.partial(kernel, nrow, ncol), out_shape=(pltpu.VM...  60.6 us
    unnamed x2, local copies, waits for them, and re-layouts  1.99 us

profile of v4, /device:TPU:17, one launch (start us, length us, event | category | flops | bytes accessed | tf_op | source)
XLA Modules:
  0.0 63.3 jit_solution(13660566527211837730)
XLA Ops:
  0.6 60.6 %shard_map.77 = (f32[1536,384]{1,0:T(8,128)S(1)}, f32[384]{0:T(512)S(1)}) custom-call(bf16[2,512,384]{2,1,0:T(8,128)(2,1)} %basis_ref.1, f32[384]{0:T(512)} %params_ref.1, f32[4,16]{1,0:T(4,128)} %values_ref.1, s32[2,16]{1,0:T(2,128)} %codes_ref.1, f32[1536,384]{1,0:T(8,128)} %prev_ref.1, f32[384]{0:T(512)} %rhs_prev_ref.1), custom_call_target="tpu_custom_call" | custom-call | tf_op jit(solution)/shard_map/pallas_call | solution.py:406
  61.3 1.4 %copy.10 = f32[1536,384]{1,0:T(8,128)} copy(f32[1536,384]{1,0:T(8,128)S(1)} %get-tuple-element.2) | data formatting | bytes 4718592
  62.7 0.6 copy.11

commit v5 on v4

--- a/solution.py
+++ b/solution.py
@@ -276,6 +276,14 @@
         count = len(groups) * quarter
         rows = count + (SIDE if groups[0] == 0 else 0)
         first = first_row(groups[0])
+        if groups[-1] == 3:
+            lhs = design[first : first + rows]
+            away[groups[0] * quarter : groups[0] * quarter + count] = lax.dot_general(
+                lhs, weighted[1], NT, preferred_element_type=f32
+            )
+            swap(groups).start()
+            collect(groups, core, lax.dot_general(lhs, weighted[0], NT, preferred_element_type=f32))
+            return
         both = weighted[...].reshape(2 * width, total)
         product = lax.dot_general(design[first : first + rows], both, NT, preferred_element_type=f32)
         away[groups[0] * quarter : groups[0] * quarter + count] = product[:count, width:]
@@ -320,6 +328,7 @@
         copy.start()
     some(build_own, 3, 4)
     pass_y(0)
+    build_rows((0,), (0,))
     for copy in g2:
         copy.wait_recv()
     amount = tot1[...]
@@ -330,7 +339,7 @@
     for copy in g3:
         copy.start()
     pass_y(1)
-    build_rows((0,), (0, 1))
+    build_rows((0,), (1,))
     pass_on(0)
     for copy in g3:
         copy.wait_recv()

time: 63.4 us -> 62.5 us (0.986); the launches traced: 63.3 us -> 61.6 us
  Pallas kernels: 60.6 us -> 59 us
    pallas_call x1, Pallas kernels: 60.6 us -> 59 us  [local(): pl.pallas_call(functools.partial(kernel, nrow, ncol), out_shape=(pltpu.VM...]
where the time goes in v5:
time: 62.5 us; the launch traced here: 61.6 us
  Pallas kernels  59 us (94%)
  local copies, waits for them, and re-layouts  1.99 us (3%)
  between operations  0.64 us (1%)
    pallas_call x1, Pallas kernels, local(): pl.pallas_call(functools.partial(kernel, nrow, ncol), out_shape=(pltpu.VM...  59 us
    unnamed x2, local copies, waits for them, and re-layouts  1.99 us

profile of v5, /device:TPU:17, one launch (start us, length us, event | category | flops | bytes accessed | tf_op | source)
XLA Modules:
  0.0 61.6 jit_solution(9109825051610200365)
XLA Ops:
  0.6 59.0 %shard_map.77 = (f32[1536,384]{1,0:T(8,128)S(1)}, f32[384]{0:T(512)S(1)}) custom-call(bf16[2,512,384]{2,1,0:T(8,128)(2,1)} %basis_ref.1, f32[384]{0:T(512)} %params_ref.1, f32[4,16]{1,0:T(4,128)} %values_ref.1, s32[2,16]{1,0:T(2,128)} %codes_ref.1, f32[1536,384]{1,0:T(8,128)} %prev_ref.1, f32[384]{0:T(512)} %rhs_prev_ref.1), custom_call_target="tpu_custom_call" | custom-call | tf_op jit(solution)/shard_map/pallas_call | solution.py:415
  59.6 1.4 %copy.10 = f32[1536,384]{1,0:T(8,128)} copy(f32[1536,384]{1,0:T(8,128)S(1)} %get-tuple-element.2) | data formatting | bytes 4718592
  61.0 0.6 copy.11

commit v6 on v5

--- a/solution.py
+++ b/solution.py
@@ -161,7 +161,7 @@
         copy.start()
 
     def pass_zx(u):
-        for d in range(1, nz):
+        for d in sorted(range(1, nz), key=lambda d: 2 * d == nz):
             for m in range(share):
                 here = half(zbuf.at[d, m], u)
                 remote(here, here, z_send.at[d, m, u], z_recv.at[d, m, u], hand[d]).wait_recv()

time: 62.5 us -> 62.8 us (level)
  no operation moved by 1% of the time
where the time goes in v6:
time: 62.8 us; the launch traced here: 61.9 us
  Pallas kernels  59.3 us (94%)
  local copies, waits for them, and re-layouts  1.99 us (3%)
  between operations  0.64 us (1%)
    pallas_call x1, Pallas kernels, local(): pl.pallas_call(functools.partial(kernel, nrow, ncol), out_shape=(pltpu.VM...  59.3 us
    unnamed x2, local copies, waits for them, and re-layouts  1.99 us

profile of v6, /device:TPU:17, one launch (start us, length us, event | category | flops | bytes accessed | tf_op | source)
XLA Modules:
  0.0 61.9 jit_solution(758911914331270949)
XLA Ops:
  0.6 59.3 %shard_map.77 = (f32[1536,384]{1,0:T(8,128)S(1)}, f32[384]{0:T(512)S(1)}) custom-call(bf16[2,512,384]{2,1,0:T(8,128)(2,1)} %basis_ref.1, f32[384]{0:T(512)} %params_ref.1, f32[4,16]{1,0:T(4,128)} %values_ref.1, s32[2,16]{1,0:T(2,128)} %codes_ref.1, f32[1536,384]{1,0:T(8,128)} %prev_ref.1, f32[384]{0:T(512)} %rhs_prev_ref.1), custom_call_target="tpu_custom_call" | custom-call | tf_op jit(solution)/shard_map/pallas_call | solution.py:415
  59.9 1.4 %copy.10 = f32[1536,384]{1,0:T(8,128)} copy(f32[1536,384]{1,0:T(8,128)S(1)} %get-tuple-element.2) | data formatting | bytes 4718592
  61.3 0.6 copy.11
